TPU v7x, 256 devices: a whole 4x4x8 slice. The times are simulated.
256 devices in a mesh: rows: 16 (over z_hi, x), cols: 4 (over z_lo, core), depth: 4 (over y).
Axes of the slice: x: 4, y: 4, z: 8 (z_hi: 4, z_lo: 2; z = z_hi * 2 + z_lo), core: 2. Of those that a mesh axis runs over, the one named last changes fastest.
Arguments:
- tokens_in: bfloat16 [256, 8192], P('rows', 'depth'), may hold values from -6 to 6
- cotangent: bfloat16 [256, 8192], P('rows', 'depth'), may hold values from -1.5 to 1.5
- w_gate: bfloat16 [8192, 28672], P('depth', ('rows', 'cols')), may hold values from -0.0625 to 0.0625
- w_up: bfloat16 [8192, 28672], P('depth', ('rows', 'cols')), may hold values from -0.0625 to 0.0625
- w_down: bfloat16 [28672, 8192], P(('rows', 'cols'), 'depth'), may hold values from -0.03125 to 0.03125
Outputs:
- block_out: bfloat16 [256, 8192], P(('rows', 'cols'), 'depth')
- input_grad: bfloat16 [256, 8192], P(('rows', 'cols'), 'depth')
- gate_grad: bfloat16 [8192, 28672], P('depth', ('rows', 'cols'))
- up_grad: bfloat16 [8192, 28672], P('depth', ('rows', 'cols'))
- down_grad: bfloat16 [28672, 8192], P(('rows', 'cols'), 'depth')
All inputs are finite; a program needn't handle non-finite values.
Results may differ from a plain program's by a relative error of at most 0.0049.
Values may be sent and summed in bfloat16 or wider, within the bound.
A program may use at most 64 MiB of HBM per device.

v0:
```python
import jax
import jax.numpy as jnp
from jax import lax
from jax.sharding import PartitionSpec as P


def backward_local(hidden_back, gate, up):
    sigma = jax.nn.sigmoid(gate)
    up_back = (hidden_back * gate * sigma).astype(jnp.bfloat16)
    gate_back = (hidden_back * up * sigma * (1.0 + gate * (1.0 - sigma))).astype(jnp.bfloat16)
    return (gate_back, up_back)


def contract_last(left, right):
    return lax.dot_general(
        left, right, (((1,), (1,)), ((), ())), preferred_element_type=jnp.float32
    )


def contract_first(left, right):
    return lax.dot_general(
        left, right, (((0,), (0,)), ((), ())), preferred_element_type=jnp.float32
    )


def on_device(tokens_in, cotangent, w_gate, w_up, w_down):
    tokens_full, cotangent_full = (
        lax.all_gather(tokens_in, "rows", axis=0, tiled=True),
        lax.all_gather(cotangent, "rows", axis=0, tiled=True),
    )
    gate_part = jnp.dot(tokens_full, w_gate, preferred_element_type=jnp.float32)
    up_part = jnp.dot(tokens_full, w_up, preferred_element_type=jnp.float32)
    gate, up = lax.psum((gate_part, up_part), "depth")
    hidden = (jax.nn.silu(gate) * up).astype(jnp.bfloat16)
    output_sum = lax.psum_scatter(
        jnp.dot(hidden, w_down, preferred_element_type=jnp.float32),
        ("rows", "cols"),
        scatter_dimension=0,
        tiled=True,
    )
    block_out = output_sum.astype(jnp.bfloat16)
    back_part = contract_last(cotangent_full, w_down)
    hidden_back = lax.psum(back_part, "depth")
    gate_back, up_back = backward_local(hidden_back, gate, up)
    input_grad = lax.psum_scatter(
        contract_last(gate_back, w_gate) + contract_last(up_back, w_up),
        ("rows", "cols"),
        scatter_dimension=0,
        tiled=True,
    ).astype(jnp.bfloat16)
    gate_grad = contract_first(tokens_full, gate_back).astype(jnp.bfloat16)
    up_grad = contract_first(tokens_full, up_back).astype(jnp.bfloat16)
    down_grad = contract_first(hidden, cotangent_full).astype(jnp.bfloat16)
    return (block_out, input_grad, gate_grad, up_grad, down_grad)


def solution(mesh):
    return jax.shard_map(
        on_device,
        mesh=mesh,
        in_specs=(
            P("rows", "depth"),
            P("rows", "depth"),
            P("depth", ("rows", "cols")),
            P("depth", ("rows", "cols")),
            P(("rows", "cols"), "depth"),
        ),
        out_specs=(
            P(("rows", "cols"), "depth"),
            P(("rows", "cols"), "depth"),
            P("depth", ("rows", "cols")),
            P("depth", ("rows", "cols")),
            P(("rows", "cols"), "depth"),
        ),
        check_vma=False,
    )
```

profile of v0, /device:TPU:1, one launch (start us, length us, event | category | flops | bytes accessed | tf_op | source)
XLA Modules:
  0.0 487.0 jit_solution(15707571623628139926)
XLA Ops:
  7.2 0.0 copy-start
  7.2 0.0 all-gather.3.cloned.1.call-start
  7.2 0.7 all-gather.3.cloned.1.call-update
  7.9 0.0 all-gather.5.cloned.1.call-start
  8.0 0.7 all-gather.5.cloned.1.call-update
  8.7 0.0 all-reduce.7.cloned.1.call-start
  8.7 57.8 %all-gather.3.cloned.1.call-done = bf16[256,2048]{1,0:T(8,128)(2,1)} async-done(((bf16[16,2048]{1,0:T(8,128)(2,1)}), bf16[256,2048]{1,0:T(8,128)(2,1)}) %all-gather.3.cloned.1.call-update) | async-done | bytes 1048592 | tf_op jit(solution)/shard_map/all_gather | solution.py:28
  66.5 0.0 copy-done
  66.6 2.8 fusion.2
  69.4 0.0 copy-done.1
  69.4 0.0 copy-done.2
  69.4 1.4 fusion.3
  70.8 48.9 %all-gather.5.cloned.1.call-done = bf16[256,2048]{1,0:T(8,128)(2,1)} async-done(((bf16[16,2048]{1,0:T(8,128)(2,1)}), bf16[256,2048]{1,0:T(8,128)(2,1)}) %all-gather.5.cloned.1.call-update) | async-done | bytes 1048592 | tf_op jit(solution)/shard_map/all_gather | solution.py:29
  119.8 3.3 fusion.5
  123.0 0.0 all-reduce.7.cloned.1.call-update
  123.1 0.0 copy-done.7
  123.1 0.6 dynamic-slice
  124.3 50.4 %all-reduce.7.cloned.1.call-done = (f32[256,448]{0,1:T(8,128)}, f32[256,448]{0,1:T(8,128)}, f32[256,448]{0,1:T(8,128)}) async-done(((f32[256,448]{0,1:T(8,128)}, f32[256,448]{0,1:T(8,128)}, f32[256,448]{0,1:T(8,128)}), (f32[256,448]{0,1:T(8,128)}, f32[256,448]{0,1:T(8,128)}, f32[256,448]{0,1:T(8,128)})) %all-reduce.7.cloned.1.call-update) | async-done | bytes 1376272 | tf_op jit(solution)/shard_map/psum | solution.py:33
  174.7 1.5 multiply_convert_fusion
  176.2 0.0 copy-start.6
  176.2 0.0 copy-start.3
  176.3 0.7 fusion.6
  177.0 0.0 copy-done.6
  177.0 0.8 copy-done.3
  177.8 2.1 convolution_add_fusion
  179.9 0.0 copy-done.4
  179.9 2.1 fusion.4
  182.0 290.5 %all-reduce.8 = (bf16[256,2048]{1,0:T(8,128)(2,1)}, bf16[256,2048]{1,0:T(8,128)(2,1)}) all-reduce(f32[256,2048]{1,0:T(8,128)} %fusion.4, f32[256,2048]{1,0:T(8,128)} %convolution_add_fusion), channel_id=2, replica_groups=mesh['rows'=16,'cols'=4,'depth'=4] {'rows','cols'}, use_global_device_ids=true, to_apply=%region_2.3.clone | all-reduce | flops 1048576 | bytes 6291456
  472.5 1.4 dynamic-slice_convert_fusion
  473.9 2.8 fusion
  476.7 1.9 fusion.1
  478.6 1.9 convolution_convert_fusion
  (6 shorter events, 0.0 us)
Async XLA Ops:
  7.2 59.4 %copy-start = (bf16[2048,448]{0,1:T(8,128)(2,1)S(1)}, bf16[2048,448]{0,1:T(8,128)(2,1)}, u32[]{:S(2)}) copy-start(bf16[2048,448]{0,1:T(8,128)(2,1)} %param.7) | copy-start | bytes 5505028
  7.2 59.4 %all-gather.3.cloned.1.call-start = ((), (), s32[]{:S(2)}) async-start(), calls=%async_computation | async-start | bytes 1114112 | tf_op jit(solution)/shard_map/all_gather | solution.py:28
  7.9 111.8 %all-gather.5.cloned.1.call-start = ((), (), s32[]{:S(2)}) async-start(), calls=%async_computation.1 | async-start | bytes 1114112 | tf_op jit(solution)/shard_map/all_gather | solution.py:29
  8.7 166.0 %all-reduce.7.cloned.1.call-start = ((), (), s32[]{:S(2)}) async-start(), calls=%async_computation.2 | async-start | bytes 2752512 | tf_op jit(solution)/shard_map/psum | solution.py:33
  66.5 2.8 copy-start.1
  66.5 2.8 copy-start.2
  70.8 52.2 %copy-start.7 = (u32[256]{0:T(256)S(1)}, u32[256]{0:T(256)}, u32[]{:S(2)}) copy-start(u32[256]{0:T(256)} %constant.6) | copy-start | bytes 3076
  176.2 0.8 copy-start.6
  176.2 1.6 copy-start.3
  177.8 2.1 copy-start.4
  476.7 1.9 copy-start.5
Sparse Core Ops, SparseCore 0:
  10.4 56.0 all-gather.2
  69.0 50.7 all-gather.4
  123.2 51.4 all-reduce.6
where the time goes:
time: 491 us; the launch traced here: 487 us
  blocking collectives  291 us (59%)
  waiting for transfers between devices  159 us (32%)
  matrix products  18.9 us (4%)
  between operations  14.5 us (3%)
    unnamed x1, blocking collectives  291 us
    all_gather x1, waiting for transfers between devices, on_device(): lax.all_gather(tokens_in, 'rows', axis=0, tiled=True)  57.8 us
    psum x1, waiting for transfers between devices, on_device(): gate, up = lax.psum((gate_part, up_part), 'depth')  50.4 us
    all_gather x1, waiting for transfers between devices, on_device(): lax.all_gather(cotangent, 'rows', axis=0, tiled=True)  48.9 us
  transfers between devices with their start and end apart: 3, of which 3 were waited for; matrix products, arithmetic and copies ran while one was open for 1% of the time, Pallas kernels for 0%

commit v1 on v0

v1 whole, which is shorter than its diff:
```python
import functools

import jax
import jax.numpy as jnp
from jax import lax
from jax.experimental import pallas as pl
from jax.experimental.pallas import tpu as pltpu
from jax.sharding import PartitionSpec as P

MESH = pl.DeviceIdType.MESH
F32 = jnp.float32
BF16 = jnp.bfloat16
NQ = 4
NX = 4
NY = 4
NC = 2
QC = NQ // NC
ROWS = 16


def contract_last(left, right):
    return lax.dot_general(
        left, right, (((1,), (1,)), ((), ())), preferred_element_type=F32
    )


def contract_first(left, right):
    return lax.dot_general(
        left, right, (((0,), (0,)), ((), ())), preferred_element_type=F32
    )


def block_kernel(
    tokens_ref, cot_ref, w_gate_ref, w_up_ref, w_down_ref,
    out_ref, back_ref, tok_out, act_out,
    tok, wg, wu, wd, part32, part16, part_in, act,
    core_send, core_in, own, xsend, xin, zown, zsend, zin, fin,
    load_sem, zs, zr, xs, xr, cs, cr, ys, yr, hs, hr, os_, or_, us, ur, vs, vr, fs, fr, st_sem,
):
    r, c, y = lax.axis_index("rows"), lax.axis_index("cols"), lax.axis_index("depth")
    z_hi, x = r // NX, r % NX
    z_lo, core = c // 2, c % 2
    half = tok.shape[-1]
    f = wg.shape[-1]
    quarter = half // 2

    def at(dz=0, dx=0, lo=None, k=None, dy=0):
        lo = z_lo if lo is None else lo
        k = core if k is None else k
        row = lax.rem(z_hi + dz, NQ) * NX + lax.rem(x + dx, NX)
        return (row, lo * 2 + k, lax.rem(y + dy, NY))

    loads = []
    for h in range(2):
        place = pl.multiple_of((core + h) % 2 * half, half)
        loads.append([
            pltpu.make_async_copy(w_gate_ref.at[pl.ds(place, half), :], wg.at[h], load_sem.at[h, 0]),
            pltpu.make_async_copy(w_up_ref.at[pl.ds(place, half), :], wu.at[h], load_sem.at[h, 1]),
            pltpu.make_async_copy(w_down_ref.at[:, pl.ds(place, half)], wd.at[h], load_sem.at[h, 2]),
        ])
    for group in loads:
        for load in group:
            load.start()

    barrier = pltpu.get_barrier_semaphore()
    partners = [at(dx=d) for d in range(1, NX)] + [at(dy=d) for d in range(1, NY)]
    partners += [at(dz=d, lo=lo) for d in range(1, NQ) for lo in range(2)]
    partners += [at(lo=1 - z_lo), at(k=1 - core), at(lo=1 - z_lo, k=1 - core)]
    for partner in partners:
        pl.semaphore_signal(barrier, inc=1, device_id=partner, device_id_type=MESH)

    mine = pl.ds(pl.multiple_of(core * half, half), half)
    tok[0, 0, 0, 0:ROWS] = tokens_ref[:, mine]
    tok[0, 1, 0, 0:ROWS] = cot_ref[:, mine]
    pl.semaphore_wait(barrier, len(partners))

    sends = []

    def send(src, dst, ss, rs, to):
        copy = pltpu.make_async_remote_copy(
            src_ref=src, dst_ref=dst, send_sem=ss, recv_sem=rs, device_id=to, device_id_type=MESH
        )
        copy.start()
        sends.append(copy)

    def arrived(dst, ss, rs, to):
        pltpu.make_async_remote_copy(
            src_ref=dst, dst_ref=dst, send_sem=ss, recv_sem=rs, device_id=to, device_id_type=MESH
        ).wait_recv()

    shift = 1 + 2 * (1 - z_lo)
    slot = 4 - shift
    own_shard = tok.at[0, :, 0, pl.ds(0, ROWS)]
    for lo in range(2):
        send(own_shard, tok.at[0, :, slot, pl.ds(0, ROWS)], zs.at[lo], zr.at[slot], at(dz=shift, lo=lo))
    send(own_shard, tok.at[0, :, 2, pl.ds(0, ROWS)], zs.at[2], zr.at[2], at(dz=2, lo=1 - z_lo))

    def stage_x(q):
        if q:
            arrived(tok.at[0, :, q, pl.ds(0, ROWS)], zs.at[0], zr.at[q], at(dx=1))
        for d in range(1, NX):
            p = NX - d
            send(
                tok.at[0, :, q, pl.ds(0, ROWS)], tok.at[0, :, q, pl.ds(p * ROWS, ROWS)],
                xs.at[q, d], xr.at[q, p], at(dx=d),
            )

    def stage_core(q):
        for p in range(1, NX):
            arrived(tok.at[0, :, q, pl.ds(p * ROWS, ROWS)], xs.at[q, p], xr.at[q, p], at(dx=1))
        send(tok.at[0, :, q], tok.at[1, :, q], cs.at[q], cr.at[q], at(k=1 - core))

    rows = QC * NX * ROWS
    share = rows // NY

    def stage_mm(n):
        gs = pl.ds(n * QC, QC)
        sums = []
        for h in range(2):
            if n == 0:
                for load in loads[h]:
                    load.wait()
            if h:
                for q in range(n * QC, n * QC + QC):
                    arrived(tok.at[1, :, q], cs.at[q], cr.at[q], at(k=1 - core))
            t = tok[h, 0, gs].reshape(rows, half)
            g = tok[h, 1, gs].reshape(rows, half)
            terms = [
                jnp.dot(t, wg[h], preferred_element_type=F32),
                jnp.dot(t, wu[h], preferred_element_type=F32),
                contract_last(g, wd[h]),
            ]
            for i, term in enumerate(terms):
                term = term.reshape(NY, share, f)
                if h:
                    term = term + part32[n, :, i]
                    part16[n, :, i] = term.astype(BF16)
                part32[n, :, i] = term
        for d in range(1, NY):
            to = lax.rem(y + d, NY)
            send(part16.at[n, to], part_in.at[n, NY - d - 1], ys.at[n, d], yr.at[n, NY - d], at(dy=d))

    def stage_act(n):
        for p in range(1, NY):
            arrived(part_in.at[n, p - 1], ys.at[n, p], yr.at[n, p], at(dy=1))
        gate, up, hidden_back = [
            part32[n, y, i] + (part_in[n, 0, i].astype(F32) + part_in[n, 1, i].astype(F32)
                               + part_in[n, 2, i].astype(F32))
            for i in range(3)
        ]
        sigma = jax.nn.sigmoid(gate)
        act[n, y, 0] = (gate * sigma * up).astype(BF16)
        act[n, y, 1] = (hidden_back * up * sigma * (1.0 + gate * (1.0 - sigma))).astype(BF16)
        act[n, y, 2] = (hidden_back * gate * sigma).astype(BF16)
        for d in range(1, NY):
            send(act.at[n, y], act.at[n, y], hs.at[n, d], hr.at[n, NY - d], at(dy=d))

    def stage_out(n):
        for p in range(1, NY):
            arrived(act.at[n, lax.rem(y + p, NY)], hs.at[n, p], hr.at[n, p], at(dy=1))
        hidden, gate_back, up_back = [act[n, :, i].reshape(rows, f) for i in range(3)]

        def outputs(h):
            return [
                jnp.dot(hidden, wd[h], preferred_element_type=F32),
                contract_last(gate_back, wg[h]) + contract_last(up_back, wu[h]),
            ]

        for i, value in enumerate(outputs(1)):
            core_send[n, i] = value.astype(core_send.dtype)
        send(core_send.at[n], core_in.at[n], os_.at[n], or_.at[n], at(k=1 - core))
        values = outputs(0)
        arrived(core_in.at[n], os_.at[n], or_.at[n], at(k=1 - core))
        for i, value in enumerate(values):
            value = (value + core_in[n, i].astype(F32)).reshape(QC, NX, ROWS, half)
            own[n, i] = value[:, 0]
            for p in range(1, NX):
                xsend[n, p - 1, i] = value[:, p].astype(BF16)
        for d in range(1, NX):
            send(xsend.at[n, d - 1], xin.at[n, NX - d - 1], us.at[n, d], ur.at[n, NX - d], at(dx=d))

    def stage_z(n):
        for p in range(1, NX):
            arrived(xin.at[n, p - 1], us.at[n, p], ur.at[n, p], at(dx=1))
        for i in range(2):
            value = own[n, i] + (xin[n, 0, i].astype(F32) + xin[n, 1, i].astype(F32) + xin[n, 2, i].astype(F32))
            for j in range(QC):
                for lo in range(2):
                    part = value[j, :, lo * quarter:(lo + 1) * quarter]
                    if n == 0 and j == 0:
                        zown[lo, i] = part
                    zsend[n * QC + j, lo, i] = part.astype(BF16)
        for j in range(QC):
            q = n * QC + j
            if q == 0:
                send(zsend.at[0, 1 - z_lo], zin.at[0, z_lo], vs.at[0, 0], vr.at[0, z_lo], at(lo=1 - z_lo))
            else:
                for lo in range(2):
                    send(zsend.at[q, lo], zin.at[NQ - q, z_lo], vs.at[q, lo], vr.at[NQ - q, z_lo], at(dz=q, lo=lo))

    def last():
        total = [zown[z_lo, i] for i in range(2)]
        arrived(zin.at[0, 1 - z_lo], vs.at[0, 0], vr.at[0, 1 - z_lo], at(lo=1 - z_lo))
        for i in range(2):
            total[i] = total[i] + zin[0, 1 - z_lo, i].astype(F32)
        for q in range(1, NQ):
            for lo in range(2):
                arrived(zin.at[q, lo], vs.at[q, lo], vr.at[q, lo], at(dz=1, lo=lo))
                for i in range(2):
                    total[i] = total[i] + zin[q, lo, i].astype(F32)
        place = core * 2 + z_lo
        for i in range(2):
            fin[place, i] = total[i].astype(BF16)
        others = [(1 - z_lo, core), (z_lo, 1 - core), (1 - z_lo, 1 - core)]
        for n, (lo, k) in enumerate(others):
            send(fin.at[place], fin.at[place], fs.at[n], fr.at[n], at(lo=lo, k=k))
        for n, (lo, k) in enumerate(others):
            arrived(fin.at[k * 2 + lo], fs.at[n], fr.at[n], at(lo=lo, k=k))
        step = ROWS // 4
        for i, ref in enumerate((out_ref, back_ref)):
            for j in range(4):
                value = fin[j, i].astype(F32)
                pick = value[0:step]
                for k in range(1, 4):
                    pick = jnp.where(c == k, value[k * step:(k + 1) * step], pick)
                ref[:, j * quarter:(j + 1) * quarter] = pick.astype(BF16)

    order = [0, 1, 3, 2]
    for q in order:
        stage_x(q)
    for q in order[:QC]:
        stage_core(q)
    stage_mm(0)
    for q in order[QC:]:
        stage_core(q)
    stage_act(0)
    stage_mm(1)
    stores = []
    for h in range(2):
        for i in range(2):
            stores.append(pltpu.make_async_copy(tok.at[h, i], tok_out.at[i, (core + h) % 2], st_sem.at[h, i]))
    for store in stores:
        store.start()
    stage_out(0)
    stage_act(1)
    stage_z(0)
    stage_out(1)
    for n in range(NC):
        stores.append(pltpu.make_async_copy(act.at[n], act_out.at[n], st_sem.at[2, n]))
        stores[-1].start()
    stage_z(1)
    last()
    for copy in sends:
        copy.wait_send()
    for store in stores:
        store.wait()


def on_device(tokens_in, cotangent, w_gate, w_up, w_down):
    d, f = w_gate.shape
    half, quarter = d // 2, d // 4
    group = NX * ROWS
    share = QC * group // NY
    tokens = NQ * group
    dma = pltpu.SemaphoreType.DMA
    vmem = pl.BlockSpec(memory_space=pltpu.VMEM)
    anywhere = pl.BlockSpec(memory_space=pl.ANY)
    out, back, tok, act = pl.pallas_call(
        block_kernel,
        out_shape=[
            jax.ShapeDtypeStruct((4, d), BF16),
            jax.ShapeDtypeStruct((4, d), BF16),
            jax.ShapeDtypeStruct((2, 2, NQ, group, half), BF16),
            jax.ShapeDtypeStruct((NC, NY, 3, share, f), BF16),
        ],
        in_specs=[vmem, vmem, anywhere, anywhere, anywhere],
        out_specs=[vmem, vmem, anywhere, anywhere],
        scratch_shapes=[
            pltpu.VMEM((2, 2, NQ, group, half), BF16),
            pltpu.VMEM((2, half, f), BF16),
            pltpu.VMEM((2, half, f), BF16),
            pltpu.VMEM((2, f, half), BF16),
            pltpu.VMEM((NC, NY, 3, share, f), F32),
            pltpu.VMEM((NC, NY, 3, share, f), BF16),
            pltpu.VMEM((NC, NY - 1, 3, share, f), BF16),
            pltpu.VMEM((NC, NY, 3, share, f), BF16),
            pltpu.VMEM((NC, 2, QC * group, half), BF16),
            pltpu.VMEM((NC, 2, QC * group, half), BF16),
            pltpu.VMEM((NC, 2, QC, ROWS, half), F32),
            pltpu.VMEM((NC, NX - 1, 2, QC, ROWS, half), BF16),
            pltpu.VMEM((NC, NX - 1, 2, QC, ROWS, half), BF16),
            pltpu.VMEM((2, 2, ROWS, quarter), F32),
            pltpu.VMEM((NQ, 2, 2, ROWS, quarter), BF16),
            pltpu.VMEM((NQ, 2, 2, ROWS, quarter), BF16),
            pltpu.VMEM((4, 2, ROWS, quarter), BF16),
            dma((2, 3)),
            dma((3,)), dma((NQ,)),
            dma((NQ, NX)), dma((NQ, NX)),
            dma((NQ,)), dma((NQ,)),
            dma((NC, NY)), dma((NC, NY)),
            dma((NC, NY)), dma((NC, NY)),
            dma((NC,)), dma((NC,)),
            dma((NC, NX)), dma((NC, NX)),
            dma((NQ, 2)), dma((NQ, 2)),
            dma((3,)), dma((3,)),
            dma((3, 2)),
        ],
        compiler_params=pltpu.CompilerParams(
            collective_id=0, has_side_effects=True, vmem_limit_bytes=40 * 2**20
        ),
        cost_estimate=pl.CostEstimate(flops=12 * tokens * d * f, bytes_accessed=6 * d * f, transcendentals=tokens * f),
        name="block",
    )(tokens_in, cotangent, w_gate, w_up, w_down)
    tok = tok.reshape(2, 2, tokens, half)
    act = jnp.moveaxis(act, 2, 0).reshape(3, tokens, f)
    hidden, gate_back, up_back = act[0], act[1], act[2]
    tokens_full = jnp.concatenate([tok[0, 0], tok[0, 1]], axis=1)
    cotangent_full = jnp.concatenate([tok[1, 0], tok[1, 1]], axis=1)
    gate_grad = contract_first(tokens_full, gate_back).astype(BF16)
    up_grad = contract_first(tokens_full, up_back).astype(BF16)
    down_grad = contract_first(hidden, cotangent_full).astype(BF16)
    return (out, back, gate_grad, up_grad, down_grad)


def solution(mesh):
    return jax.shard_map(
        on_device,
        mesh=mesh,
        in_specs=(
            P("rows", "depth"),
            P("rows", "depth"),
            P("depth", ("rows", "cols")),
            P("depth", ("rows", "cols")),
            P(("rows", "cols"), "depth"),
        ),
        out_specs=(
            P(("rows", "cols"), "depth"),
            P(("rows", "cols"), "depth"),
            P("depth", ("rows", "cols")),
            P("depth", ("rows", "cols")),
            P(("rows", "cols"), "depth"),
        ),
        check_vma=False,
    )
```

time: 491 us -> 89.8 us (0.18)
  blocking collectives: 291 us -> 0 us
  waiting for transfers between devices: 159 us -> 0 us
  Pallas kernels: 0 us -> 71.9 us
  between operations: 14.5 us -> 0.69 us
  matrix products: 18.9 us -> 5.74 us
  local copies, waits for them, and re-layouts: 2.86 us -> 11.3 us
    unnamed x1 -> x0, blocking collectives: 291 us -> none
    all_gather x2 -> x0, waiting for transfers between devices: 107 us -> none  [the longest x1 57.8 us: on_device(): lax.all_gather(tokens_in, 'rows', axis=0, tiled=True)]
    pallas_call x0 -> x1, Pallas kernels: none -> 71.9 us  [on_device(): pl.pallas_call(block_kernel, out_shape=[jax.ShapeDtypeStruct((4, d), BF16...]
    psum x1 -> x0, waiting for transfers between devices: 50.4 us -> none  [on_device(): gate, up = lax.psum((gate_part, up_part), 'depth')]
    dot_general x6 -> x0, matrix products: 12.4 us -> none  [the longest x3 6.06 us: contract_last(): lax.dot_general(left, right, (((1,), (1,)), ((), ())), preferred_element_...]
    unnamed x17 -> x12, local copies, waits for them, and re-layouts: 1.45 us -> 11 us
  transfers between devices with their start and end apart: 3 -> 0, of which waited for: 3 -> 0; matrix products, arithmetic and copies ran while one was open for 1% -> 0% of each run, Pallas kernels for 0% -> 0%
where the time goes in v1:
time: 89.8 us; the launch traced here: 89.6 us
  Pallas kernels  71.9 us (80%)
  local copies, waits for them, and re-layouts  11.3 us (13%)
  matrix products  5.74 us (6%)
    pallas_call x1, Pallas kernels, on_device(): pl.pallas_call(block_kernel, out_shape=[jax.ShapeDtypeStruct((4, d), BF16...  71.9 us
    unnamed x12, local copies, waits for them, and re-layouts  11 us
    dot_general x3, matrix products, contract_first(): lax.dot_general(left, right, (((0,), (0,)), ((), ())), preferred_element_...  5.74 us

profile of v1, /device:TPU:1, one launch (start us, length us, event | category | flops | bytes accessed | tf_op | source)
XLA Modules:
  0.0 89.6 jit_solution(17364872624220556763)
XLA Ops:
  0.6 2.8 %copy.10.w_gate_ref = bf16[2048,448]{1,0:T(8,128)(2,1)S(1)} copy(bf16[2048,448]{0,1:T(8,128)(2,1)} %param.7) | data formatting | bytes 3670016 | tf_op args[2]
  3.4 0.0 copy-start.2
  3.5 0.0 copy-start.3
  3.5 3.9 %copy.11.w_up_ref = bf16[2048,448]{1,0:T(8,128)(2,1)} copy(bf16[2048,448]{0,1:T(8,128)(2,1)} %param.8) | data formatting | bytes 3670016 | tf_op args[3]
  7.3 0.0 copy-done.2
  7.3 0.0 copy-done.3
  7.3 0.0 copy-start
  7.3 1.6 %copy-done = bf16[2048,448]{1,0:T(8,128)(2,1)S(1)} copy-done((bf16[2048,448]{1,0:T(8,128)(2,1)S(1)}, bf16[2048,448]{1,0:T(8,128)(2,1)}, u32[]{:S(2)}) %copy-start) | copy-done | bytes 1835032
  8.9 0.0 copy-start.1
  8.9 1.5 %copy-done.1 = bf16[448,2048]{1,0:T(8,128)(2,1)S(1)} copy-done((bf16[448,2048]{1,0:T(8,128)(2,1)S(1)}, bf16[448,2048]{1,0:T(8,128)(2,1)}, u32[]{:S(2)}) %copy-start.1) | copy-done | bytes 1835032
  10.4 71.9 %block.1 = (bf16[4,2048]{1,0:T(4,128)(2,1)S(1)}, bf16[4,2048]{1,0:T(4,128)(2,1)S(1)}, bf16[2,2,4,64,1024]{4,3,2,1,0:T(8,128)(2,1)S(1)}, bf16[2,4,3,32,448]{4,3,2,1,0:T(8,128)(2,1)S(1)}) custom-call(bf16[16,2048]{1,0:T(8,128)(2,1)S(1)} %copy-done.2, bf16[16,2048]{1,0:T(8,128)(2,1)S(1)} %copy-done.3, bf16[2048,448]{1,0:T(8,128)(2,1)S(1)} %copy.10.w_gate_ref, ...), custom_call_target="tpu_custom_call" | custom-call | flops 2818572288 | bytes 5505024 | tf_op jit(solution)/shard_map/block/pallas_call | solution.py:268
  82.3 0.1 fusion.6
  82.4 0.2 slice_bitcast_fusion.1
  82.6 1.9 %convolution_convert_fusion = bf16[448,2048]{1,0:T(8,128)(2,1)} fusion(bf16[256,448]{1,0:T(8,128)(2,1)S(1)} %bitcast.18, bf16[256,1024]{1,0:T(8,128)(2,1)S(1)} %get-tuple-element.14, bf16[256,1024]{1,0:T(8,128)(2,1)S(1)} %get-tuple-element.13), kind=kOutput, calls=%fused_computation | convolution fusion | flops 472776704 | bytes 3112960 | tf_op jit(solution)/shard_map/dot_general | solution.py:28
  84.5 1.9 %convolution_convert_fusion.1 = bf16[2048,448]{0,1:T(8,128)(2,1)} fusion(bf16[256,448]{1,0:T(8,128)(2,1)S(1)} %bitcast.20, bf16[256,1024]{1,0:T(8,128)(2,1)S(1)} %get-tuple-element.15, bf16[256,1024]{1,0:T(8,128)(2,1)S(1)} %get-tuple-element.16), kind=kOutput, calls=%fused_computation.1 | convolution fusion | flops 472776704 | bytes 3112960 | tf_op jit(solution)/shard_map/dot_general | solution.py:28
  86.4 1.9 %convolution_convert_fusion.2 = bf16[2048,448]{0,1:T(8,128)(2,1)} fusion(bf16[256,448]{1,0:T(8,128)(2,1)S(1)} %bitcast.19, bf16[256,1024]{1,0:T(8,128)(2,1)S(1)} %get-tuple-element.15, bf16[256,1024]{1,0:T(8,128)(2,1)S(1)} %get-tuple-element.16), kind=kOutput, calls=%fused_computation.2 | convolution fusion | flops 472776704 | bytes 3112960 | tf_op jit(solution)/shard_map/dot_general | solution.py:28
  88.3 0.6 copy.14
  88.9 0.6 copy.15
Async XLA Ops:
  3.4 3.9 %copy-start.2 = (bf16[16,2048]{1,0:T(8,128)(2,1)S(1)}, bf16[16,2048]{1,0:T(8,128)(2,1)}, u32[]{:S(2)}) copy-start(bf16[16,2048]{1,0:T(8,128)(2,1)} %tokens_ref.1) | copy-start | bytes 196612
  3.5 3.9 %copy-start.3 = (bf16[16,2048]{1,0:T(8,128)(2,1)S(1)}, bf16[16,2048]{1,0:T(8,128)(2,1)}, u32[]{:S(2)}) copy-start(bf16[16,2048]{1,0:T(8,128)(2,1)} %cot_ref.1) | copy-start | bytes 196612
  7.3 1.6 %copy-start = (bf16[2048,448]{1,0:T(8,128)(2,1)S(1)}, bf16[2048,448]{1,0:T(8,128)(2,1)}, u32[]{:S(2)}) copy-start(bf16[2048,448]{1,0:T(8,128)(2,1)} %copy.11.w_up_ref) | copy-start | bytes 5505028
  8.9 1.5 %copy-start.1 = (bf16[448,2048]{1,0:T(8,128)(2,1)S(1)}, bf16[448,2048]{1,0:T(8,128)(2,1)}, u32[]{:S(2)}) copy-start(bf16[448,2048]{1,0:T(8,128)(2,1)} %w_down_ref.1) | copy-start | bytes 5505028

commit v2 on v1

--- a/solution.py
+++ b/solution.py
@@ -22,6 +22,10 @@
     return lax.dot_general(
         left, right, (((1,), (1,)), ((), ())), preferred_element_type=F32
     )
+
+
+def matmul(left, right):
+    return jnp.dot(left, right, preferred_element_type=F32)
 
 
 def contract_first(left, right):
@@ -41,7 +45,7 @@
     z_hi, x = r // NX, r % NX
     z_lo, core = c // 2, c % 2
     half = tok.shape[-1]
-    f = wg.shape[-1]
+    f = wg.shape[1]
     quarter = half // 2
 
     def at(dz=0, dx=0, lo=None, k=None, dy=0):
@@ -54,9 +58,8 @@
     for h in range(2):
         place = pl.multiple_of((core + h) % 2 * half, half)
         loads.append([
-            pltpu.make_async_copy(w_gate_ref.at[pl.ds(place, half), :], wg.at[h], load_sem.at[h, 0]),
-            pltpu.make_async_copy(w_up_ref.at[pl.ds(place, half), :], wu.at[h], load_sem.at[h, 1]),
-            pltpu.make_async_copy(w_down_ref.at[:, pl.ds(place, half)], wd.at[h], load_sem.at[h, 2]),
+            pltpu.make_async_copy(ref.at[:, pl.ds(place, half)], held.at[h], load_sem.at[h, i])
+            for i, (ref, held) in enumerate(((w_gate_ref, wg), (w_up_ref, wu), (w_down_ref, wd)))
         ])
     for group in loads:
         for load in group:
@@ -126,8 +129,8 @@
             t = tok[h, 0, gs].reshape(rows, half)
             g = tok[h, 1, gs].reshape(rows, half)
             terms = [
-                jnp.dot(t, wg[h], preferred_element_type=F32),
-                jnp.dot(t, wu[h], preferred_element_type=F32),
+                contract_last(t, wg[h]),
+                contract_last(t, wu[h]),
                 contract_last(g, wd[h]),
             ]
             for i, term in enumerate(terms):
@@ -162,8 +165,8 @@
 
         def outputs(h):
             return [
-                jnp.dot(hidden, wd[h], preferred_element_type=F32),
-                contract_last(gate_back, wg[h]) + contract_last(up_back, wu[h]),
+                matmul(hidden, wd[h]),
+                matmul(gate_back, wg[h]) + matmul(up_back, wu[h]),
             ]
 
         for i, value in enumerate(outputs(1)):
@@ -238,7 +241,8 @@
     stores = []
     for h in range(2):
         for i in range(2):
-            stores.append(pltpu.make_async_copy(tok.at[h, i], tok_out.at[i, (core + h) % 2], st_sem.at[h, i]))
+            place = pl.ds(pl.multiple_of((core + h) % 2 * half, half), half)
+            stores.append(pltpu.make_async_copy(tok.at[h, i], tok_out.at[i, :, :, place], st_sem.at[h, i]))
     for store in stores:
         store.start()
     stage_out(0)
@@ -246,14 +250,51 @@
     stage_z(0)
     stage_out(1)
     for n in range(NC):
-        stores.append(pltpu.make_async_copy(act.at[n], act_out.at[n], st_sem.at[2, n]))
-        stores[-1].start()
+        for i in range(3):
+            stores.append(pltpu.make_async_copy(act.at[n, :, i], act_out.at[i, n], st_sem.at[2 + n, i]))
+            stores[-1].start()
     stage_z(1)
     last()
     for copy in sends:
         copy.wait_send()
     for store in stores:
         store.wait()
+
+
+def grads_kernel(out_ref, back_ref, tok_ref, act_ref, out_copy, back_copy, gate_grad, up_grad, down_grad):
+    @pl.when(pl.program_id(0) == 0)
+    def _():
+        out_copy[...] = out_ref[...]
+        back_copy[...] = back_ref[...]
+
+    f = act_ref.shape[-1]
+    tokens, cot = [tok_ref[i].reshape(-1, tok_ref.shape[-1]) for i in range(2)]
+    hidden, gate_back, up_back = [act_ref[i].reshape(-1, f) for i in range(3)]
+    gate_grad[...] = contract_first(gate_back, tokens).astype(BF16)
+    up_grad[...] = contract_first(up_back, tokens).astype(BF16)
+    down_grad[...] = contract_first(hidden, cot).astype(BF16)
+
+
+def weight_grads(out, back, tok, act):
+    d, f = tok.shape[-1], act.shape[-1]
+    tile = 512
+    whole = pl.BlockSpec(out.shape, lambda i: (0, 0))
+    grad = pl.BlockSpec((f, tile), lambda i: (0, i))
+    small = jax.ShapeDtypeStruct(out.shape, BF16)
+    large = jax.ShapeDtypeStruct((f, d), BF16)
+    return pl.pallas_call(
+        grads_kernel,
+        grid=(d // tile,),
+        out_shape=[small, small, large, large, large],
+        in_specs=[
+            whole, whole,
+            pl.BlockSpec(tok.shape[:-1] + (tile,), lambda i: (0,) * (tok.ndim - 1) + (i,)),
+            pl.BlockSpec(act.shape, lambda i: (0,) * act.ndim),
+        ],
+        out_specs=[whole, whole, grad, grad, grad],
+        compiler_params=pltpu.CompilerParams(vmem_limit_bytes=56 * 2**20),
+        name="grads",
+    )(out, back, tok, act)
 
 
 def on_device(tokens_in, cotangent, w_gate, w_up, w_down):
@@ -265,20 +306,21 @@
     dma = pltpu.SemaphoreType.DMA
     vmem = pl.BlockSpec(memory_space=pltpu.VMEM)
     anywhere = pl.BlockSpec(memory_space=pl.ANY)
+    hbm = pl.BlockSpec(memory_space=pltpu.HBM)
     out, back, tok, act = pl.pallas_call(
         block_kernel,
         out_shape=[
             jax.ShapeDtypeStruct((4, d), BF16),
             jax.ShapeDtypeStruct((4, d), BF16),
-            jax.ShapeDtypeStruct((2, 2, NQ, group, half), BF16),
-            jax.ShapeDtypeStruct((NC, NY, 3, share, f), BF16),
+            jax.ShapeDtypeStruct((2, NQ, group, d), BF16),
+            jax.ShapeDtypeStruct((3, NC, NY, share, f), BF16),
         ],
-        in_specs=[vmem, vmem, anywhere, anywhere, anywhere],
+        in_specs=[vmem, vmem, hbm, hbm, hbm],
         out_specs=[vmem, vmem, anywhere, anywhere],
         scratch_shapes=[
             pltpu.VMEM((2, 2, NQ, group, half), BF16),
-            pltpu.VMEM((2, half, f), BF16),
-            pltpu.VMEM((2, half, f), BF16),
+            pltpu.VMEM((2, f, half), BF16),
+            pltpu.VMEM((2, f, half), BF16),
             pltpu.VMEM((2, f, half), BF16),
             pltpu.VMEM((NC, NY, 3, share, f), F32),
             pltpu.VMEM((NC, NY, 3, share, f), BF16),
@@ -303,23 +345,16 @@
             dma((NC, NX)), dma((NC, NX)),
             dma((NQ, 2)), dma((NQ, 2)),
             dma((3,)), dma((3,)),
-            dma((3, 2)),
+            dma((2 + NC, 3)),
         ],
         compiler_params=pltpu.CompilerParams(
-            collective_id=0, has_side_effects=True, vmem_limit_bytes=40 * 2**20
+            collective_id=0, has_side_effects=True, vmem_limit_bytes=56 * 2**20
         ),
         cost_estimate=pl.CostEstimate(flops=12 * tokens * d * f, bytes_accessed=6 * d * f, transcendentals=tokens * f),
         name="block",
-    )(tokens_in, cotangent, w_gate, w_up, w_down)
-    tok = tok.reshape(2, 2, tokens, half)
-    act = jnp.moveaxis(act, 2, 0).reshape(3, tokens, f)
-    hidden, gate_back, up_back = act[0], act[1], act[2]
-    tokens_full = jnp.concatenate([tok[0, 0], tok[0, 1]], axis=1)
-    cotangent_full = jnp.concatenate([tok[1, 0], tok[1, 1]], axis=1)
-    gate_grad = contract_first(tokens_full, gate_back).astype(BF16)
-    up_grad = contract_first(tokens_full, up_back).astype(BF16)
-    down_grad = contract_first(hidden, cotangent_full).astype(BF16)
-    return (out, back, gate_grad, up_grad, down_grad)
+    )(tokens_in, cotangent, w_gate.T, w_up.T, w_down)
+    out, back, gate_grad, up_grad, down_grad = weight_grads(out, back, tok, act)
+    return (out, back, gate_grad.T, up_grad.T, down_grad)
 
 
 def solution(mesh):

time: 89.8 us -> 78.4 us (0.87)
  local copies, waits for them, and re-layouts: 11.3 us -> 0 us
  matrix products: 5.74 us -> 0 us
  Pallas kernels: 71.9 us -> 77.5 us
    unnamed x12 -> x0, local copies, waits for them, and re-layouts: 11 us -> none
    dot_general x3 -> x0, matrix products: 5.74 us -> none  [contract_first(): lax.dot_general(left, right, (((0,), (0,)), ((), ())), preferred_element_...]
    pallas_call x0 -> x1, Pallas kernels: none -> 5.51 us  [weight_grads(): pl.pallas_call(grads_kernel, grid=(d // tile,), out_shape=[small, small,...]
where the time goes in v2:
time: 78.4 us; the launch traced here: 78.2 us
  Pallas kernels  77.5 us (99%)
    pallas_call x1, Pallas kernels, on_device(): pl.pallas_call(block_kernel, out_shape=[jax.ShapeDtypeStruct((4, d), BF16...  72 us
    pallas_call x1, Pallas kernels, weight_grads(): pl.pallas_call(grads_kernel, grid=(d // tile,), out_shape=[small, small,...  5.51 us

profile of v2, /device:TPU:1, one launch (start us, length us, event | category | flops | bytes accessed | tf_op | source)
XLA Modules:
  0.0 78.2 jit_solution(14199086455671349517)
XLA Ops:
  0.6 72.0 %block.1 = (bf16[4,2048]{1,0:T(4,128)(2,1)}, bf16[4,2048]{1,0:T(4,128)(2,1)}, bf16[2,4,64,2048]{3,2,1,0:T(8,128)(2,1)}, bf16[3,2,4,32,448]{4,3,2,1,0:T(8,128)(2,1)}) custom-call(bf16[16,2048]{1,0:T(8,128)(2,1)} %tokens_ref.1, bf16[16,2048]{1,0:T(8,128)(2,1)} %cot_ref.1, bf16[448,2048]{1,0:T(8,128)(2,1)} %bitcast.4, bf16[448,2048]{1,0:T(8,128)(2,1)} %bitcast.5, ...), custom_call_target="tpu_custom_call" | custom-call | flops 2818572288 | bytes 5505024 | tf_op jit(solution)/shard_map/block/pallas_call | solution.py:310
  72.6 5.5 %grads.1 = (bf16[4,2048]{1,0:T(4,128)(2,1)}, bf16[4,2048]{1,0:T(4,128)(2,1)}, bf16[448,2048]{1,0:T(8,128)(2,1)}, bf16[448,2048]{1,0:T(8,128)(2,1)}, bf16[448,2048]{1,0:T(8,128)(2,1)}) custom-call(bf16[4,2048]{1,0:T(4,128)(2,1)} %get-tuple-element.14.out_ref, bf16[4,2048]{1,0:T(4,128)(2,1)} %get-tuple-element.15.back_ref, ...), custom_call_target="tpu_custom_call" | custom-call | tf_op jit(solution)/shard_map/grads/pallas_call | solution.py:285

commit v3 on v2

v3 whole, which is shorter than its diff:
```python
import functools

import jax
import jax.numpy as jnp
from jax import lax
from jax.experimental import pallas as pl
from jax.experimental.pallas import tpu as pltpu
from jax.sharding import PartitionSpec as P

MESH = pl.DeviceIdType.MESH
F32 = jnp.float32
BF16 = jnp.bfloat16
NQ = 4
NX = 4
NY = 4
ORDER = [0, 1, 3, 2]
ROWS = 16


def contract_last(left, right):
    return lax.dot_general(
        left, right, (((1,), (1,)), ((), ())), preferred_element_type=F32
    )


def matmul(left, right):
    return jnp.dot(left, right, preferred_element_type=F32)


def contract_first(left, right):
    return lax.dot_general(
        left, right, (((0,), (0,)), ((), ())), preferred_element_type=F32
    )


def block_kernel(
    tokens_ref, cot_ref, w_gate_ref, w_up_ref, w_down_ref,
    out_ref, back_ref, tok_out, act_out,
    tok, held, other, part32, part16, part_in, act, act_other,
    own, xsend, xin, zf, zsend, zin,
    load_sem, ws, wr, zs, zr, xs, xr, fs, fr, cs, cr, ys, yr, hs, hr, ks, kr, us, ur, vs, vr, st_sem,
):
    r, c, y = lax.axis_index("rows"), lax.axis_index("cols"), lax.axis_index("depth")
    z_hi, x = r // NX, r % NX
    z_lo, core = c // 2, c % 2
    half = tok.shape[-1]
    f = held.shape[2]
    piece = half // 4
    weights = (w_gate_ref, w_up_ref, w_down_ref)

    def at(dz=0, dx=0, lo=None, k=None, dy=0):
        lo = z_lo if lo is None else lo
        k = core if k is None else k
        row = lax.rem(z_hi + dz, NQ) * NX + lax.rem(x + dx, NX)
        return (row, lo * 2 + k, lax.rem(y + dy, NY))

    def features(h):
        return pl.ds(pl.multiple_of((core + h) % 2 * half, half), half)

    loads = [
        [
            pltpu.make_async_copy(ref.at[:, features(h)], held.at[h, i], load_sem.at[h, i])
            for i, ref in enumerate(weights)
        ]
        for h in range(2)
    ]
    for group in loads:
        for load in group:
            load.start()

    barrier = pltpu.get_barrier_semaphore()
    neighbour = at(k=1 - core)
    group = [(1 - z_lo, core), (z_lo, 1 - core), (1 - z_lo, 1 - core)]
    partners = [at(dx=d) for d in range(1, NX)] + [at(dy=d) for d in range(1, NY)]
    partners += [at(dz=d, lo=lo, k=k) for d in range(1, NQ) for lo in range(2) for k in range(2)]
    partners += [at(lo=lo, k=k) for lo, k in group]
    for partner in partners:
        pl.semaphore_signal(barrier, inc=1, device_id=partner, device_id_type=MESH)

    tok[0, 0, 0, 0:ROWS] = tokens_ref[:, features(0)]
    tok[0, 1, 0, 0:ROWS] = cot_ref[:, features(0)]
    pl.semaphore_wait(barrier, len(partners))

    sends = []

    def send(src, dst, ss, rs, to):
        copy = pltpu.make_async_remote_copy(
            src_ref=src, dst_ref=dst, send_sem=ss, recv_sem=rs, device_id=to, device_id_type=MESH
        )
        copy.start()
        sends.append(copy)

    def arrived(dst, ss, rs):
        pltpu.make_async_remote_copy(
            src_ref=dst, dst_ref=dst, send_sem=ss, recv_sem=rs, device_id=neighbour, device_id_type=MESH
        ).wait_recv()

    def shard(q, p):
        return tok.at[0, :, q, pl.ds(p * ROWS, ROWS)]

    shift = 1 + 2 * (1 - z_lo)
    slot = 4 - shift

    def stage_x(q):
        if q:
            arrived(shard(q, 0), zs.at[0], zr.at[q])
        for d in (1, NX - 1):
            send(shard(q, 0), shard(q, NX - d), xs.at[q, d], xr.at[q, NX - d], at(dx=d))

    def stage_pass(q):
        for i, p in enumerate((NX - 1, 1)):
            arrived(shard(q, p), xs.at[q, p], xr.at[q, p])
            send(
                tok.at[0, i, q, pl.ds(p * ROWS, ROWS)], tok.at[0, i, q, pl.ds(2 * ROWS, ROWS)],
                fs.at[q, i], fr.at[q, i], at(dx=NX - p),
            )

    def stage_core(q):
        for i in range(2):
            arrived(tok.at[0, i, q, pl.ds(2 * ROWS, ROWS)], fs.at[q, i], fr.at[q, i])
        send(tok.at[0, :, q], tok.at[1, :, q], cs.at[q], cr.at[q], neighbour)

    def stage_weight(i):
        send(weights[i].at[:, features(1)], other.at[i], ws.at[i], wr.at[i], neighbour)

    rows = NX * ROWS
    share = rows // NY

    def stage_mm(n):
        for h in range(2):
            if n == 0:
                for load in loads[h]:
                    load.wait()
            if h:
                arrived(tok.at[1, :, n], cs.at[n], cr.at[n])
            for i in range(3):
                term = contract_last(tok[h, i // 2, n], held[h, i]).reshape(NY, share, f)
                if h:
                    term = term + part32[n, :, i]
                    part16[n, :, i] = term.astype(BF16)
                part32[n, :, i] = term
        for d in (1, 3, 2):
            to = lax.rem(y + d, NY)
            send(part16.at[n, to], part_in.at[n, NY - d - 1], ys.at[n, d], yr.at[n, NY - d], at(dy=d))

    def stage_act(n):
        for p in range(1, NY):
            arrived(part_in.at[n, p - 1], ys.at[n, p], yr.at[n, p])
        gate, up, hidden_back = [
            part32[n, y, i] + (part_in[n, 0, i].astype(F32) + part_in[n, 1, i].astype(F32)
                               + part_in[n, 2, i].astype(F32))
            for i in range(3)
        ]
        sigma = jax.nn.sigmoid(gate)
        act[n, y, 0] = (gate * sigma * up).astype(BF16)
        act[n, y, 1] = (hidden_back * up * sigma * (1.0 + gate * (1.0 - sigma))).astype(BF16)
        act[n, y, 2] = (hidden_back * gate * sigma).astype(BF16)
        for d in (1, 3, 2):
            send(act.at[n, y], act.at[n, y], hs.at[n, d], hr.at[n, NY - d], at(dy=d))
        send(act.at[n, y], act_other.at[n, y], ks.at[n, 0], kr.at[n, 0], neighbour)

    def stage_out(n):
        for p in (1, 3, 2):
            place = lax.rem(y + p, NY)
            arrived(act.at[n, place], hs.at[n, p], hr.at[n, p])
            send(act.at[n, place], act_other.at[n, place], ks.at[n, p], kr.at[n, p], neighbour)

        def outputs(ref, w):
            hidden, gate_back, up_back = [ref[n, :, i].reshape(rows, f) for i in range(3)]
            return [matmul(hidden, w[2]), matmul(gate_back, w[0]) + matmul(up_back, w[1])]

        mine = outputs(act, held.at[0])
        if n == 0:
            for i in range(3):
                arrived(other.at[i], ws.at[i], wr.at[i])
        for p in range(NY):
            arrived(act_other.at[n, lax.rem(y + p, NY)], ks.at[n, p], kr.at[n, p])
        for i, (left, right) in enumerate(zip(mine, outputs(act_other, other))):
            value = (left + right).reshape(NX, ROWS, half)
            own[n, i] = value[0]
            for p in range(1, NX):
                xsend[n, p - 1, i] = value[p].astype(BF16)
        for d in (1, 3, 2):
            send(xsend.at[n, d - 1], xin.at[n, NX - d - 1], us.at[n, d], ur.at[n, NX - d], at(dx=d))

    def stage_z(n):
        for p in range(1, NX):
            arrived(xin.at[n, p - 1], us.at[n, p], ur.at[n, p])
        step = ROWS // 4
        for i in range(2):
            value = own[n, i] + (xin[n, 0, i].astype(F32) + xin[n, 1, i].astype(F32) + xin[n, 2, i].astype(F32))
            for k in range(4):
                for j in range(4):
                    zf[n, k, i, j * step:(j + 1) * step] = value[k * step:(k + 1) * step, j * piece:(j + 1) * piece]
                zsend[n, k, i] = zf[n, k, i].astype(BF16)
        back = (NQ - n) % NQ
        for lo, k in group if n == 0 else [(0, 0), (0, 1), (1, 0), (1, 1)]:
            to = lo * 2 + k
            send(zsend.at[n, to], zin.at[back, c], vs.at[n, to], vr.at[back, c], at(dz=n, lo=lo, k=k))

    def last():
        zin[0, c] = zsend[0, c]
        sums = [[None, None], [None, None]]
        for lo, k in group:
            to = lo * 2 + k
            arrived(zin.at[0, to], vs.at[0, to], vr.at[0, to])
        for q in ORDER:
            for to in range(4):
                if q:
                    arrived(zin.at[q, to], vs.at[q, to], vr.at[q, to])
                for i in range(2):
                    value = zin[q, to, i].astype(F32)
                    if q == 0:
                        value = jnp.where(c == to, zf[0, to, i], value)
                    total = sums[to % 2][i]
                    sums[to % 2][i] = value if total is None else total + value
        step = ROWS // 4
        for i, ref in enumerate((out_ref, back_ref)):
            for k in range(2):
                for j in range(4):
                    ref[:, k * half + j * piece:k * half + (j + 1) * piece] = (
                        sums[k][i][j * step:(j + 1) * step].astype(BF16)
                    )

    stores = []

    def store_tokens():
        for h in range(2):
            for i in range(2):
                stores.append(pltpu.make_async_copy(tok.at[h, i], tok_out.at[i, :, :, features(h)], st_sem.at[h, i]))
                stores[-1].start()

    def store_act(n):
        for i in range(3):
            stores.append(pltpu.make_async_copy(act.at[n, :, i], act_out.at[i, n], st_sem.at[2 + n, i]))
            stores[-1].start()

    for lo in range(2):
        send(shard(0, 0), shard(slot, 0), zs.at[lo], zr.at[slot], at(dz=shift, lo=lo))
    send(shard(0, 0), shard(2, 0), zs.at[2], zr.at[2], at(dz=2, lo=1 - z_lo))
    stage_x(0)
    stage_x(1)
    stage_x(3)
    stage_pass(0)
    stage_x(2)
    stage_pass(1)
    stage_core(0)
    stage_pass(3)
    stage_mm(0)
    stage_pass(2)
    stage_core(1)
    stage_weight(0)
    stage_core(3)
    stage_weight(1)
    stage_mm(1)
    stage_act(0)
    stage_core(2)
    stage_weight(2)
    stage_mm(3)
    stage_act(1)
    stage_mm(2)
    store_tokens()
    stage_out(0)
    stage_act(3)
    stage_out(1)
    stage_act(2)
    stage_z(0)
    stage_out(3)
    stage_z(1)
    stage_out(2)
    for n in ORDER:
        store_act(n)
    stage_z(3)
    stage_z(2)
    last()
    for copy in sends:
        copy.wait_send()
    for store in stores:
        store.wait()


def grads_kernel(out_ref, back_ref, tok_ref, act_ref, out_copy, back_copy, gate_grad, up_grad, down_grad):
    @pl.when(pl.program_id(0) == 0)
    def _():
        out_copy[...] = out_ref[...]
        back_copy[...] = back_ref[...]

    f = act_ref.shape[-1]
    tokens, cot = [tok_ref[i].reshape(-1, tok_ref.shape[-1]) for i in range(2)]
    hidden, gate_back, up_back = [act_ref[i].reshape(-1, f) for i in range(3)]
    gate_grad[...] = contract_first(gate_back, tokens).astype(BF16)
    up_grad[...] = contract_first(up_back, tokens).astype(BF16)
    down_grad[...] = contract_first(hidden, cot).astype(BF16)


def weight_grads(out, back, tok, act):
    d, f = tok.shape[-1], act.shape[-1]
    tile = 512
    whole = pl.BlockSpec(out.shape, lambda i: (0, 0))
    grad = pl.BlockSpec((f, tile), lambda i: (0, i))
    small = jax.ShapeDtypeStruct(out.shape, BF16)
    large = jax.ShapeDtypeStruct((f, d), BF16)
    return pl.pallas_call(
        grads_kernel,
        grid=(d // tile,),
        out_shape=[small, small, large, large, large],
        in_specs=[
            whole, whole,
            pl.BlockSpec(tok.shape[:-1] + (tile,), lambda i: (0,) * (tok.ndim - 1) + (i,)),
            pl.BlockSpec(act.shape, lambda i: (0,) * act.ndim),
        ],
        out_specs=[whole, whole, grad, grad, grad],
        compiler_params=pltpu.CompilerParams(vmem_limit_bytes=56 * 2**20),
        name="grads",
    )(out, back, tok, act)


def on_device(tokens_in, cotangent, w_gate, w_up, w_down):
    d, f = w_gate.shape
    half = d // 2
    piece = half // 4
    group = NX * ROWS
    share = group // NY
    tokens = NQ * group
    dma = pltpu.SemaphoreType.DMA
    vmem = pl.BlockSpec(memory_space=pltpu.VMEM)
    hbm = pl.BlockSpec(memory_space=pltpu.HBM)
    out, back, tok, act = pl.pallas_call(
        block_kernel,
        out_shape=[
            jax.ShapeDtypeStruct((4, d), BF16),
            jax.ShapeDtypeStruct((4, d), BF16),
            jax.ShapeDtypeStruct((2, NQ, group, d), BF16),
            jax.ShapeDtypeStruct((3, NQ, NY, share, f), BF16),
        ],
        in_specs=[vmem, vmem, hbm, hbm, hbm],
        out_specs=[vmem, vmem, hbm, hbm],
        scratch_shapes=[
            pltpu.VMEM((2, 2, NQ, group, half), BF16),
            pltpu.VMEM((2, 3, f, half), BF16),
            pltpu.VMEM((3, f, half), BF16),
            pltpu.VMEM((NQ, NY, 3, share, f), F32),
            pltpu.VMEM((NQ, NY, 3, share, f), BF16),
            pltpu.VMEM((NQ, NY - 1, 3, share, f), BF16),
            pltpu.VMEM((NQ, NY, 3, share, f), BF16),
            pltpu.VMEM((NQ, NY, 3, share, f), BF16),
            pltpu.VMEM((NQ, 2, ROWS, half), F32),
            pltpu.VMEM((NQ, NX - 1, 2, ROWS, half), BF16),
            pltpu.VMEM((NQ, NX - 1, 2, ROWS, half), BF16),
            pltpu.VMEM((NQ, 4, 2, ROWS, piece), F32),
            pltpu.VMEM((NQ, 4, 2, ROWS, piece), BF16),
            pltpu.VMEM((NQ, 4, 2, ROWS, piece), BF16),
            dma((2, 3)),
            dma((3,)), dma((3,)),
            dma((3,)), dma((NQ,)),
            dma((NQ, NX)), dma((NQ, NX)),
            dma((NQ, 2)), dma((NQ, 2)),
            dma((NQ,)), dma((NQ,)),
            dma((NQ, NY)), dma((NQ, NY)),
            dma((NQ, NY)), dma((NQ, NY)),
            dma((NQ, NY)), dma((NQ, NY)),
            dma((NQ, NX)), dma((NQ, NX)),
            dma((NQ, 4)), dma((NQ, 4)),
            dma((2 + NQ, 3)),
        ],
        compiler_params=pltpu.CompilerParams(
            collective_id=0, has_side_effects=True, vmem_limit_bytes=56 * 2**20
        ),
        cost_estimate=pl.CostEstimate(flops=12 * tokens * d * f, bytes_accessed=6 * d * f, transcendentals=tokens * f),
        name="block",
    )(tokens_in, cotangent, w_gate.T, w_up.T, w_down)
    out, back, gate_grad, up_grad, down_grad = weight_grads(out, back, tok, act)
    return (out, back, gate_grad.T, up_grad.T, down_grad)


def solution(mesh):
    return jax.shard_map(
        on_device,
        mesh=mesh,
        in_specs=(
            P("rows", "depth"),
            P("rows", "depth"),
            P("depth", ("rows", "cols")),
            P("depth", ("rows", "cols")),
            P(("rows", "cols"), "depth"),
        ),
        out_specs=(
            P(("rows", "cols"), "depth"),
            P(("rows", "cols"), "depth"),
            P("depth", ("rows", "cols")),
            P("depth", ("rows", "cols")),
            P(("rows", "cols"), "depth"),
        ),
        check_vma=False,
    )
```

time: 78.4 us -> 68.5 us (0.87)
  Pallas kernels: 77.5 us -> 67.7 us
    pallas_call x1, Pallas kernels: 72 us -> 62.2 us  [on_device(): pl.pallas_call(block_kernel, out_shape=[jax.ShapeDtypeStruct((4, d), BF16...]
where the time goes in v3:
time: 68.5 us; the launch traced here: 68.3 us
  Pallas kernels  67.7 us (99%)
    pallas_call x1, Pallas kernels, on_device(): pl.pallas_call(block_kernel, out_shape=[jax.ShapeDtypeStruct((4, d), BF16...  62.2 us
    pallas_call x1, Pallas kernels, weight_grads(): pl.pallas_call(grads_kernel, grid=(d // tile,), out_shape=[small, small,...  5.51 us

profile of v3, /device:TPU:1, one launch (start us, length us, event | category | flops | bytes accessed | tf_op | source)
XLA Modules:
  0.0 68.3 jit_solution(4653218142033571108)
XLA Ops:
  0.6 62.2 %block.1 = (bf16[4,2048]{1,0:T(4,128)(2,1)}, bf16[4,2048]{1,0:T(4,128)(2,1)}, bf16[2,4,64,2048]{3,2,1,0:T(8,128)(2,1)}, bf16[3,4,4,16,448]{4,3,2,1,0:T(8,128)(2,1)}) custom-call(bf16[16,2048]{1,0:T(8,128)(2,1)} %tokens_ref.1, bf16[16,2048]{1,0:T(8,128)(2,1)} %cot_ref.1, bf16[448,2048]{1,0:T(8,128)(2,1)} %bitcast.4, bf16[448,2048]{1,0:T(8,128)(2,1)} %bitcast.5, ...), custom_call_target="tpu_custom_call" | custom-call | flops 2818572288 | bytes 5505024 | tf_op jit(solution)/shard_map/block/pallas_call | solution.py:328
  62.8 5.5 %grads.1 = (bf16[4,2048]{1,0:T(4,128)(2,1)}, bf16[4,2048]{1,0:T(4,128)(2,1)}, bf16[448,2048]{1,0:T(8,128)(2,1)}, bf16[448,2048]{1,0:T(8,128)(2,1)}, bf16[448,2048]{1,0:T(8,128)(2,1)}) custom-call(bf16[4,2048]{1,0:T(4,128)(2,1)} %get-tuple-element.14.out_ref, bf16[4,2048]{1,0:T(4,128)(2,1)} %get-tuple-element.15.back_ref, ...), custom_call_target="tpu_custom_call" | custom-call | tf_op jit(solution)/shard_map/grads/pallas_call | solution.py:303

commit v4 on v3

v4 whole, which is shorter than its diff:
```python
import functools

import jax
import jax.numpy as jnp
from jax import lax
from jax.experimental import pallas as pl
from jax.experimental.pallas import tpu as pltpu
from jax.sharding import PartitionSpec as P

MESH = pl.DeviceIdType.MESH
F32 = jnp.float32
BF16 = jnp.bfloat16
NQ = 4
NX = 4
NY = 4
ORDER = [0, 1, 3, 2]
ROWS = 16


def contract_last(left, right):
    return lax.dot_general(
        left, right, (((1,), (1,)), ((), ())), preferred_element_type=F32
    )


def matmul(left, right):
    return jnp.dot(left, right, preferred_element_type=F32)


def contract_first(left, right):
    return lax.dot_general(
        left, right, (((0,), (0,)), ((), ())), preferred_element_type=F32
    )


def block_kernel(
    tokens_ref, cot_ref, w_gate_ref, w_up_ref, w_down_ref,
    out_ref, back_ref, tok_out, act_out,
    tok, held, other, part32, part16, part_in, act, act_other,
    own, xsend, xin, zf, zsend, zin,
    load_sem, store_sem, sent, wr, zr, xr, cr, yr, hr, kr, ur, vr,
):
    r, c, y = lax.axis_index("rows"), lax.axis_index("cols"), lax.axis_index("depth")
    z_hi, x = r // NX, r % NX
    z_lo, core = c // 2, c % 2
    half = tok.shape[-1]
    f = held.shape[2]
    piece = half // 4
    weights = (w_gate_ref, w_up_ref, w_down_ref)

    def at(dz=0, dx=0, lo=None, k=None, dy=0):
        lo = z_lo if lo is None else lo
        k = core if k is None else k
        row = lax.rem(z_hi + dz, NQ) * NX + lax.rem(x + dx, NX)
        return (row, lo * 2 + k, lax.rem(y + dy, NY))

    def features(h):
        return pl.ds(pl.multiple_of((core + h) % 2 * half, half), half)

    for h in range(2):
        for i, ref in enumerate(weights):
            pltpu.make_async_copy(ref.at[:, features(h)], held.at[h, i], load_sem.at[h]).start()

    barrier = pltpu.get_barrier_semaphore()
    neighbour = at(k=1 - core)
    group = [(1 - z_lo, core), (z_lo, 1 - core), (1 - z_lo, 1 - core)]
    partners = [at(dx=d) for d in range(1, NX)] + [at(dy=d) for d in range(1, NY)]
    partners += [at(dz=d, lo=lo, k=k) for d in range(1, NQ) for lo in range(2) for k in range(2)]
    partners += [at(lo=lo, k=k) for lo, k in group]
    for partner in partners:
        pl.semaphore_signal(barrier, inc=1, device_id=partner, device_id_type=MESH)

    tok[0, 0, 0, 0:ROWS] = tokens_ref[:, features(0)]
    tok[0, 1, 0, 0:ROWS] = cot_ref[:, features(0)]
    pl.semaphore_wait(barrier, len(partners))

    Z, X, CORE, WEIGHT, SUM, ACT, PASS, OUT, NEAR, FAR = range(10)

    def send(src, dst, kind, rs, to):
        pltpu.make_async_remote_copy(
            src_ref=src, dst_ref=dst, send_sem=sent.at[kind], recv_sem=rs, device_id=to, device_id_type=MESH
        ).start()

    def arrived(dst, rs):
        pltpu.make_async_remote_copy(
            src_ref=dst, dst_ref=dst, send_sem=sent.at[0], recv_sem=rs, device_id=neighbour, device_id_type=MESH
        ).wait_recv()

    def left(size, kind):
        pltpu.make_async_remote_copy(
            src_ref=size, dst_ref=size, send_sem=sent.at[kind], recv_sem=wr.at[0], device_id=neighbour, device_id_type=MESH
        ).wait_send()

    def shard(q, p):
        return tok.at[0, :, q, pl.ds(p * ROWS, ROWS)]

    shift = 1 + 2 * (1 - z_lo)
    slot = 4 - shift

    PASSED = (1, 3)

    def stage_x(q):
        if q:
            arrived(shard(q, 0), zr.at[q])
        for d in (1, 3) if q in PASSED else (1, 3, 2):
            p = NX - d
            send(shard(q, 0), shard(q, p), X, xr.at[q, p if q in PASSED else 0], at(dx=d))

    def stage_pass(q):
        for i, p in enumerate((NX - 1, 1)):
            arrived(shard(q, p), xr.at[q, p])
            here = tok.at[0, i, q, pl.ds(p * ROWS, ROWS)]
            there = tok.at[0, i, q, pl.ds(2 * ROWS, ROWS)]
            send(here, there, X, xr.at[q, 2], at(dx=NX - p))

    def stage_core(q):
        if q in PASSED:
            arrived(shard(q, 2), xr.at[q, 2])
        else:
            arrived(tok.at[0, :, q, pl.ds(ROWS, 3 * ROWS)], xr.at[q, 0])
        send(tok.at[0, :, q], tok.at[1, :, q], CORE, cr.at[q], neighbour)

    def stage_weight(i):
        send(weights[i].at[:, features(1)], other.at[i], WEIGHT, wr.at[0], neighbour)

    rows = NX * ROWS
    share = rows // NY

    def stage_mm(n, h):
        if n == 0:
            pltpu.make_async_copy(held.at[h], held.at[h], load_sem.at[h]).wait()
        if h:
            arrived(tok.at[1, :, n], cr.at[n])
        both = contract_last(tok[h, 0, n], held[h, 0:2].reshape(2 * f, half))
        back = contract_last(tok[h, 1, n], held[h, 2])
        for term, lanes in ((both, slice(0, 2 * f)), (back, slice(2 * f, 3 * f))):
            term = term.reshape(NY, share, -1)
            if h:
                term = term + part32[n, :, :, lanes]
                part16[n, :, :, lanes] = term.astype(BF16)
            part32[n, :, :, lanes] = term
        if h:
            for d in (1, 3, 2):
                to = lax.rem(y + d, NY)
                send(part16.at[n, to], part_in.at[n, NY - d - 1], SUM, yr.at[n], at(dy=d))

    def stage_act(n):
        arrived(part_in.at[n], yr.at[n])
        total = part32[n, y] + (part_in[n, 0].astype(F32) + part_in[n, 1].astype(F32) + part_in[n, 2].astype(F32))
        gate, up, hidden_back = [total[:, i * f:(i + 1) * f] for i in range(3)]
        sigma = jax.nn.sigmoid(gate)
        gate_back = hidden_back * up * sigma * (1.0 + gate * (1.0 - sigma))
        up_back = hidden_back * gate * sigma
        hidden = gate * sigma * up
        act[n, y] = jnp.concatenate([gate_back, up_back, hidden], axis=1).astype(BF16)
        for d in (1, 3, 2):
            send(act.at[n, y], act.at[n, y], ACT, hr.at[n], at(dy=d))
        send(act.at[n, y], act_other.at[n, y], PASS, kr.at[n], neighbour)

    def stage_out(n):
        arrived(part_in.at[n], hr.at[n])
        for p in (1, 3, 2):
            place = lax.rem(y + p, NY)
            send(act.at[n, place], act_other.at[n, place], PASS, kr.at[n], neighbour)

        def outputs(ref, w, i):
            if i == 0:
                return matmul(ref[n, :, :, 2 * f:].reshape(rows, f), w[2])
            return matmul(ref[n, :, :, :2 * f].reshape(rows, 2 * f), w[0:2].reshape(2 * f, half))

        mine = [outputs(act, held.at[0], i) for i in range(2)]
        if n == 0:
            arrived(other, wr.at[0])
        arrived(act_other.at[n], kr.at[n])
        for i in range(2):
            value = (mine[i] + outputs(act_other, other, i)).reshape(NX, ROWS, half)
            own[n, i] = value[0]
            xsend[n, i] = value[1:].astype(BF16)
            for d in (1, 3, 2):
                send(xsend.at[n, i, d - 1], xin.at[n, i, NX - d - 1], OUT, ur.at[n, i], at(dx=d))

    step = ROWS // 4

    def stage_z(n):
        for i in range(2):
            arrived(xin.at[n, i], ur.at[n, i])
            value = own[n, i] + (xin[n, i, 0].astype(F32) + xin[n, i, 1].astype(F32) + xin[n, i, 2].astype(F32))
            for k in range(4):
                for j in range(4):
                    zf[n, i, k, j * step:(j + 1) * step] = value[k * step:(k + 1) * step, j * piece:(j + 1) * piece]
            zsend[n, i] = zf[n, i].astype(BF16)
            if n == 0:
                for m, (lo, k) in enumerate(group):
                    send(zsend.at[0, i, lo * 2 + k], zin.at[0, i, m + 1], NEAR, vr.at[0, i], at(lo=lo, k=k))
            else:
                for lo in range(2):
                    for k in range(2):
                        send(zsend.at[n, i, lo * 2 + k], zin.at[NQ - n, i, c], FAR, vr.at[NQ - n, i], at(dz=n, lo=lo, k=k))

    def last():
        for i, ref in enumerate((out_ref, back_ref)):
            arrived(zin.at[0, i, pl.ds(1, 3)], vr.at[0, i])
            same = zf[0, i, c] + zin[0, i, 1].astype(F32)
            cross = zin[0, i, 2].astype(F32) + zin[0, i, 3].astype(F32)
            sums = [jnp.where(core == 0, same, cross), jnp.where(core == 0, cross, same)]
            for q in ORDER[1:]:
                arrived(zin.at[q, i], vr.at[q, i])
                for k in range(2):
                    sums[k] = sums[k] + (zin[q, i, k].astype(F32) + zin[q, i, 2 + k].astype(F32))
            for k in range(2):
                for j in range(4):
                    ref[:, k * half + j * piece:k * half + (j + 1) * piece] = (
                        sums[k][j * step:(j + 1) * step].astype(BF16)
                    )

    def store_tokens():
        for h in range(2):
            for i in range(2):
                pltpu.make_async_copy(tok.at[h, i], tok_out.at[i, :, :, features(h)], store_sem.at[0]).start()

    def store_act(n):
        pltpu.make_async_copy(act.at[n], act_out.at[n], store_sem.at[1]).start()

    for lo in range(2):
        send(shard(0, 0), shard(slot, 0), Z, zr.at[slot], at(dz=shift, lo=lo))
    send(shard(0, 0), shard(2, 0), Z, zr.at[2], at(dz=2, lo=1 - z_lo))
    stage_x(0)
    stage_x(1)
    stage_x(3)
    stage_core(0)
    stage_mm(0, 0)
    stage_pass(1)
    stage_mm(0, 1)
    stage_x(2)
    stage_pass(3)
    stage_core(1)
    stage_weight(0)
    stage_mm(1, 0)
    stage_core(3)
    stage_weight(1)
    stage_mm(1, 1)
    stage_mm(3, 0)
    stage_act(0)
    stage_mm(3, 1)
    stage_core(2)
    stage_weight(2)
    stage_mm(2, 0)
    stage_mm(2, 1)
    store_tokens()
    stage_act(1)
    stage_act(3)
    stage_out(0)
    stage_act(2)
    stage_out(1)
    stage_out(3)
    stage_z(0)
    stage_out(2)
    for n in ORDER:
        store_act(n)
    stage_z(1)
    stage_z(3)
    stage_z(2)
    last()
    left(tok.at[0, :, 0, pl.ds(0, 3 * ROWS)], Z)
    left(tok.at[0, :, pl.ds(0, 3)], X)
    left(tok.at[0], CORE)
    left(other, WEIGHT)
    left(part_in, SUM)
    left(part_in, ACT)
    left(act, PASS)
    left(xin, OUT)
    left(zin.at[0, :, pl.ds(1, 3)], NEAR)
    left(zin.at[pl.ds(1, 3)], FAR)
    pltpu.make_async_copy(tok, tok, store_sem.at[0]).wait()
    pltpu.make_async_copy(act, act, store_sem.at[1]).wait()


def grads_kernel(out_ref, back_ref, tok_ref, act_ref, out_copy, back_copy, gate_grad, up_grad, down_grad):
    @pl.when(pl.program_id(0) == 0)
    def _():
        out_copy[...] = out_ref[...]
        back_copy[...] = back_ref[...]

    f = act_ref.shape[-1] // 3
    tokens, cot = [tok_ref[i].reshape(-1, tok_ref.shape[-1]) for i in range(2)]
    act = act_ref[...].reshape(-1, 3 * f)
    both = contract_first(act[:, :2 * f], tokens).astype(BF16)
    gate_grad[...] = both[:f]
    up_grad[...] = both[f:]
    down_grad[...] = contract_first(act[:, 2 * f:], cot).astype(BF16)


def weight_grads(out, back, tok, act):
    d, f = tok.shape[-1], act.shape[-1] // 3
    tile = 1024
    whole = pl.BlockSpec(out.shape, lambda i: (0, 0))
    grad = pl.BlockSpec((f, tile), lambda i: (0, i))
    small = jax.ShapeDtypeStruct(out.shape, BF16)
    large = jax.ShapeDtypeStruct((f, d), BF16)
    return pl.pallas_call(
        grads_kernel,
        grid=(d // tile,),
        out_shape=[small, small, large, large, large],
        in_specs=[
            whole, whole,
            pl.BlockSpec(tok.shape[:-1] + (tile,), lambda i: (0,) * (tok.ndim - 1) + (i,)),
            pl.BlockSpec(act.shape, lambda i: (0,) * act.ndim),
        ],
        out_specs=[whole, whole, grad, grad, grad],
        compiler_params=pltpu.CompilerParams(vmem_limit_bytes=56 * 2**20),
        name="grads",
    )(out, back, tok, act)


def on_device(tokens_in, cotangent, w_gate, w_up, w_down):
    d, f = w_gate.shape
    half = d // 2
    piece = half // 4
    group = NX * ROWS
    share = group // NY
    tokens = NQ * group
    dma = pltpu.SemaphoreType.DMA
    vmem = pl.BlockSpec(memory_space=pltpu.VMEM)
    hbm = pl.BlockSpec(memory_space=pltpu.HBM)
    out, back, tok, act = pl.pallas_call(
        block_kernel,
        out_shape=[
            jax.ShapeDtypeStruct((4, d), BF16),
            jax.ShapeDtypeStruct((4, d), BF16),
            jax.ShapeDtypeStruct((2, NQ, group, d), BF16),
            jax.ShapeDtypeStruct((NQ, NY, share, 3 * f), BF16),
        ],
        in_specs=[vmem, vmem, hbm, hbm, hbm],
        out_specs=[vmem, vmem, hbm, hbm],
        scratch_shapes=[
            pltpu.VMEM((2, 2, NQ, group, half), BF16),
            pltpu.VMEM((2, 3, f, half), BF16),
            pltpu.VMEM((3, f, half), BF16),
            pltpu.VMEM((NQ, NY, share, 3 * f), F32),
            pltpu.VMEM((NQ, NY, share, 3 * f), BF16),
            pltpu.VMEM((NQ, NY - 1, share, 3 * f), BF16),
            pltpu.VMEM((NQ, NY, share, 3 * f), BF16),
            pltpu.VMEM((NQ, NY, share, 3 * f), BF16),
            pltpu.VMEM((NQ, 2, ROWS, half), F32),
            pltpu.VMEM((NQ, 2, NX - 1, ROWS, half), BF16),
            pltpu.VMEM((NQ, 2, NX - 1, ROWS, half), BF16),
            pltpu.VMEM((NQ, 2, 4, ROWS, piece), F32),
            pltpu.VMEM((NQ, 2, 4, ROWS, piece), BF16),
            pltpu.VMEM((NQ, 2, 4, ROWS, piece), BF16),
            dma((2,)),
            dma((2,)),
            dma((10,)),
            dma((1,)),
            dma((NQ,)),
            dma((NQ, NX)),
            dma((NQ,)),
            dma((NQ,)),
            dma((NQ,)),
            dma((NQ,)),
            dma((NQ, 2)),
            dma((NQ, 2)),
        ],
        compiler_params=pltpu.CompilerParams(
            collective_id=0, has_side_effects=True, vmem_limit_bytes=56 * 2**20
        ),
        cost_estimate=pl.CostEstimate(flops=12 * tokens * d * f, bytes_accessed=6 * d * f, transcendentals=tokens * f),
        name="block",
    )(tokens_in, cotangent, w_gate.T, w_up.T, w_down)
    out, back, gate_grad, up_grad, down_grad = weight_grads(out, back, tok, act)
    return (out, back, gate_grad.T, up_grad.T, down_grad)


def solution(mesh):
    return jax.shard_map(
        on_device,
        mesh=mesh,
        in_specs=(
            P("rows", "depth"),
            P("rows", "depth"),
            P("depth", ("rows", "cols")),
            P("depth", ("rows", "cols")),
            P(("rows", "cols"), "depth"),
        ),
        out_specs=(
            P(("rows", "cols"), "depth"),
            P(("rows", "cols"), "depth"),
            P("depth", ("rows", "cols")),
            P("depth", ("rows", "cols")),
            P(("rows", "cols"), "depth"),
        ),
        check_vma=False,
    )
```

time: 68.5 us -> 63.7 us (0.930)
  Pallas kernels: 67.7 us -> 62.9 us
    pallas_call x1, Pallas kernels: 62.2 us -> 58.3 us  [on_device(): pl.pallas_call(block_kernel, out_shape=[jax.ShapeDtypeStruct((4, d), BF16...]
    pallas_call x1, Pallas kernels: 5.51 us -> 4.62 us  [weight_grads(): pl.pallas_call(grads_kernel, grid=(d // tile,), out_shape=[small, small,...]
where the time goes in v4:
time: 63.7 us; the launch traced here: 63.5 us
  Pallas kernels  62.9 us (99%)
  between operations  0.64 us (1%)
    pallas_call x1, Pallas kernels, on_device(): pl.pallas_call(block_kernel, out_shape=[jax.ShapeDtypeStruct((4, d), BF16...  58.3 us
    pallas_call x1, Pallas kernels, weight_grads(): pl.pallas_call(grads_kernel, grid=(d // tile,), out_shape=[small, small,...  4.62 us

profile of v4, /device:TPU:1, one launch (start us, length us, event | category | flops | bytes accessed | tf_op | source)
XLA Modules:
  0.0 63.5 jit_solution(13624904315649893934)
XLA Ops:
  0.6 58.3 %block.1 = (bf16[4,2048]{1,0:T(4,128)(2,1)}, bf16[4,2048]{1,0:T(4,128)(2,1)}, bf16[2,4,64,2048]{3,2,1,0:T(8,128)(2,1)}, bf16[4,4,16,1344]{3,2,1,0:T(8,128)(2,1)}) custom-call(bf16[16,2048]{1,0:T(8,128)(2,1)} %tokens_ref.1, bf16[16,2048]{1,0:T(8,128)(2,1)} %cot_ref.1, bf16[448,2048]{1,0:T(8,128)(2,1)} %bitcast.4, bf16[448,2048]{1,0:T(8,128)(2,1)} %bitcast.5, ...), custom_call_target="tpu_custom_call" | custom-call | flops 2818572288 | bytes 5505024 | tf_op jit(solution)/shard_map/block/pallas_call | solution.py:325
  58.9 4.6 %grads.1 = (bf16[4,2048]{1,0:T(4,128)(2,1)}, bf16[4,2048]{1,0:T(4,128)(2,1)}, bf16[448,2048]{1,0:T(8,128)(2,1)}, bf16[448,2048]{1,0:T(8,128)(2,1)}, bf16[448,2048]{1,0:T(8,128)(2,1)}) custom-call(bf16[4,2048]{1,0:T(4,128)(2,1)} %get-tuple-element.14.out_ref, bf16[4,2048]{1,0:T(4,128)(2,1)} %get-tuple-element.15.back_ref, ...), custom_call_target="tpu_custom_call" | custom-call | tf_op jit(solution)/shard_map/grads/pallas_call | solution.py:300

commit v5 on v0

v5 whole, which is shorter than its diff:
```python
import functools

import jax
import jax.numpy as jnp
from jax import lax
from jax.experimental import pallas as pl
from jax.experimental.pallas import tpu as pltpu
from jax.sharding import PartitionSpec as P

MESH = pl.DeviceIdType.MESH
F32 = jnp.float32
BF16 = jnp.bfloat16
NQ = 4
NX = 4
NY = 4
ORDER = [0, 1, 3, 2]
ROWS = 16


def contract_last(left, right):
    return lax.dot_general(
        left, right, (((1,), (1,)), ((), ())), preferred_element_type=F32
    )


def matmul(left, right):
    return jnp.dot(left, right, preferred_element_type=F32)


def contract_first(left, right):
    return lax.dot_general(
        left, right, (((0,), (0,)), ((), ())), preferred_element_type=F32
    )


def block_kernel(
    tokens_ref, cot_ref, w_gate_ref, w_up_ref, w_down_ref,
    out_ref, back_ref, tok_out, hidden_out, backs_out,
    tok, held, other, sum_a, sum_b, part_a, part_b, in_a, in_b, act_a, act_b, other_a, other_b,
    own, xsend, xin, zf, zsend, zin,
    load_sem, store_sem, sent, wr, zr, xr, cr, yr, hr, kr, ur, vr,
):
    r, c, y = lax.axis_index("rows"), lax.axis_index("cols"), lax.axis_index("depth")
    z_hi, x = r // NX, r % NX
    z_lo, core = c // 2, c % 2
    half = tok.shape[-1]
    f = held.shape[2]
    piece = half // 4
    weights = (w_gate_ref, w_up_ref, w_down_ref)
    sums, parts, parts_in = (sum_a, sum_b), (part_a, part_b), (in_a, in_b)
    acts, acts_other, acts_out = (act_a, act_b), (other_a, other_b), (hidden_out, backs_out)

    def at(dz=0, dx=0, lo=None, k=None, dy=0):
        lo = z_lo if lo is None else lo
        k = core if k is None else k
        row = lax.rem(z_hi + dz, NQ) * NX + lax.rem(x + dx, NX)
        return (row, lo * 2 + k, lax.rem(y + dy, NY))

    def features(h):
        return pl.ds(pl.multiple_of((core + h) % 2 * half, half), half)

    for a, ref in enumerate((tokens_ref, cot_ref)):
        pltpu.make_async_copy(ref.at[:, features(0)], tok.at[0, a, 0, pl.ds(0, ROWS)], load_sem.at[2]).start()

    barrier = pltpu.get_barrier_semaphore()
    neighbour = at(k=1 - core)
    group = [(1 - z_lo, core), (z_lo, 1 - core), (1 - z_lo, 1 - core)]
    partners = [at(dx=d) for d in range(1, NX)] + [at(dy=d) for d in range(1, NY)]
    partners += [at(dz=d, lo=lo, k=k) for d in range(1, NQ) for lo in range(2) for k in range(2)]
    partners += [at(lo=lo, k=k) for lo, k in group]
    for partner in partners:
        pl.semaphore_signal(barrier, inc=1, device_id=partner, device_id_type=MESH)

    for h in range(2):
        for i, ref in enumerate(weights):
            pltpu.make_async_copy(ref.at[:, features(h)], held.at[h, i], load_sem.at[h]).start()

    own_shard = tok.at[0, :, 0, pl.ds(0, ROWS)]
    pltpu.make_async_copy(own_shard, own_shard, load_sem.at[2]).wait()
    pl.semaphore_wait(barrier, len(partners))

    Z, X, CORE, WEIGHT, SUM_A, SUM_B, ACT_A, ACT_B, PASS_A, PASS_B, OUT, NEAR, FAR = range(13)

    def send(src, dst, kind, rs, to):
        pltpu.make_async_remote_copy(
            src_ref=src, dst_ref=dst, send_sem=sent.at[kind], recv_sem=rs, device_id=to, device_id_type=MESH
        ).start()

    def arrived(dst, rs):
        pltpu.make_async_remote_copy(
            src_ref=dst, dst_ref=dst, send_sem=sent.at[0], recv_sem=rs, device_id=neighbour, device_id_type=MESH
        ).wait_recv()

    def left(size, kind):
        pltpu.make_async_remote_copy(
            src_ref=size, dst_ref=size, send_sem=sent.at[kind], recv_sem=wr.at[0], device_id=neighbour, device_id_type=MESH
        ).wait_send()

    def shard(a, q, p):
        return tok.at[0, a, q, pl.ds(p * ROWS, ROWS)]

    up = 3 - 2 * z_lo
    steps = (0, up, 2, NQ - up)

    def stage_z_in(a):
        send(shard(a, 0, 0), shard(a, 1, 0), Z, zr.at[a, 1], at(dz=up, lo=1 - z_lo))
        send(shard(a, 0, 0), shard(a, 3, 0), Z, zr.at[a, 3], at(dz=up))
        send(shard(a, 0, 0), shard(a, 2, 0), Z, zr.at[a, 2], at(dz=2, lo=1 - z_lo))

    def stage_x(a, q):
        if q:
            arrived(shard(a, q, 0), zr.at[a, q])
        for d in (1, 3, 2):
            send(shard(a, q, 0), shard(a, q, NX - d), X, xr.at[a, q], at(dx=d))

    def stage_core(a, q):
        arrived(tok.at[0, a, q, pl.ds(ROWS, 3 * ROWS)], xr.at[a, q])
        send(tok.at[0, a, q], tok.at[1, a, q], CORE, cr.at[a, q], neighbour)

    def stage_weights():
        for i in (2, 0, 1):
            send(weights[i].at[:, features(1)], other.at[i], WEIGHT, wr.at[0], neighbour)

    rows = NX * ROWS
    share = rows // NY

    def stage_mm(a, n, h):
        if n == 0 and a == 0:
            pltpu.make_async_copy(held.at[h], held.at[h], load_sem.at[h]).wait()
        if h:
            arrived(tok.at[1, a, n], cr.at[a, n])
        w = held[h, 2] if a else held[h, 0:2].reshape(2 * f, half)
        term = contract_last(tok[h, a, n], w).reshape(NY, share, -1)
        if h:
            term = term + sums[a][n]
            parts[a][n] = term.astype(BF16)
        sums[a][n] = term
        if h:
            for d in (1, 3, 2):
                to = lax.rem(y + d, NY)
                send(parts[a].at[n, to], parts_in[a].at[n, NY - d - 1], SUM_A + a, yr.at[a, n], at(dy=d))

    def stage_act(a, n):
        arrived(parts_in[a].at[n], yr.at[a, n])
        into = parts_in[a]
        total = sums[a][n, y] + (into[n, 0].astype(F32) + into[n, 1].astype(F32) + into[n, 2].astype(F32))
        if a == 0:
            sum_a[n, y] = total
            gate, up_sum = total[:, :f], total[:, f:]
            act_a[n, y] = (gate * jax.nn.sigmoid(gate) * up_sum).astype(BF16)
        else:
            gate, up_sum = sum_a[n, y, :, :f], sum_a[n, y, :, f:]
            sigma = jax.nn.sigmoid(gate)
            gate_back = total * up_sum * sigma * (1.0 + gate * (1.0 - sigma))
            act_b[n, y] = jnp.concatenate([gate_back, total * gate * sigma], axis=1).astype(BF16)
        for d in (1, 3, 2):
            send(acts[a].at[n, y], acts[a].at[n, y], ACT_A + a, hr.at[a, n], at(dy=d))
        send(acts[a].at[n, y], acts_other[a].at[n, y], PASS_A + a, kr.at[a, n], neighbour)

    def stage_out(a, n):
        arrived(parts_in[1 - a].at[n], hr.at[a, n])
        for p in (1, 3, 2):
            place = lax.rem(y + p, NY)
            send(acts[a].at[n, place], acts_other[a].at[n, place], PASS_A + a, kr.at[a, n], neighbour)

        def output(ref, w):
            left_side = ref[n].reshape(rows, -1)
            return matmul(left_side, w[0:2].reshape(2 * f, half) if a else w[2])

        mine = output(acts[a], held.at[0])
        if n == 0 and a == 0:
            arrived(other, wr.at[0])
        arrived(acts_other[a].at[n], kr.at[a, n])
        value = (mine + output(acts_other[a], other)).reshape(NX, ROWS, half)
        own[n, a] = value[0]
        xsend[n, a] = value[1:].astype(BF16)
        for d in (1, 3, 2):
            send(xsend.at[n, a, d - 1], xin.at[n, a, NX - d - 1], OUT, ur.at[a, n], at(dx=d))

    step = ROWS // 4

    def stage_z(a, n):
        arrived(xin.at[n, a], ur.at[a, n])
        value = own[n, a] + (xin[n, a, 0].astype(F32) + xin[n, a, 1].astype(F32) + xin[n, a, 2].astype(F32))
        for k in range(4):
            for j in range(4):
                zf[n, a, k, j * step:(j + 1) * step] = value[k * step:(k + 1) * step, j * piece:(j + 1) * piece]
        zsend[n, a] = zf[n, a].astype(BF16)
        if n == 0:
            for m, (lo, k) in enumerate(group):
                send(zsend.at[0, a, lo * 2 + k], zin.at[0, a, m + 1], NEAR, vr.at[a, 0], at(lo=lo, k=k))
        else:
            for differs in range(2):
                lo = 1 - z_lo if differs else z_lo
                back = 2 if n == 2 else 1 if differs == (n == 1) else 3
                for k in range(2):
                    send(zsend.at[n, a, lo * 2 + k], zin.at[back, a, c], FAR, vr.at[a, back], at(dz=steps[n], lo=lo, k=k))

    def last(a, ref):
        arrived(zin.at[0, a, pl.ds(1, 3)], vr.at[a, 0])
        same = zf[0, a, c] + zin[0, a, 1].astype(F32)
        cross = zin[0, a, 2].astype(F32) + zin[0, a, 3].astype(F32)
        totals = [jnp.where(core == 0, same, cross), jnp.where(core == 0, cross, same)]
        for q in ORDER[1:]:
            arrived(zin.at[q, a], vr.at[a, q])
            for k in range(2):
                totals[k] = totals[k] + (zin[q, a, k].astype(F32) + zin[q, a, 2 + k].astype(F32))
        for k in range(2):
            for j in range(4):
                ref[:, k * half + j * piece:k * half + (j + 1) * piece] = (
                    totals[k][j * step:(j + 1) * step].astype(BF16)
                )

    def store_tokens():
        for h in range(2):
            for i in range(2):
                pltpu.make_async_copy(tok.at[h, i], tok_out.at[i, :, :, features(h)], store_sem.at[0]).start()

    def store_acts(a):
        pltpu.make_async_copy(acts[a], acts_out[a], store_sem.at[1 + a]).start()

    stage_z_in(0)
    stage_x(0, 0)
    stage_z_in(1)
    stage_x(1, 0)
    stage_x(0, 1)
    stage_core(0, 0)
    stage_mm(0, 0, 0)
    stage_x(0, 3)
    stage_mm(0, 0, 1)
    stage_core(1, 0)
    stage_x(0, 2)
    stage_x(1, 1)
    stage_mm(1, 0, 0)
    stage_mm(1, 0, 1)
    stage_x(1, 3)
    stage_core(0, 1)
    stage_mm(0, 1, 0)
    stage_x(1, 2)
    stage_core(0, 3)
    stage_mm(0, 1, 1)
    stage_mm(0, 3, 0)
    stage_act(0, 0)
    stage_mm(0, 3, 1)
    stage_core(0, 2)
    stage_core(1, 1)
    stage_weights()
    stage_act(1, 0)
    stage_mm(0, 2, 0)
    stage_mm(0, 2, 1)
    stage_mm(1, 1, 0)
    stage_mm(1, 1, 1)
    stage_core(1, 3)
    stage_act(0, 1)
    stage_mm(1, 3, 0)
    stage_mm(1, 3, 1)
    stage_core(1, 2)
    stage_act(0, 3)
    stage_mm(1, 2, 0)
    stage_mm(1, 2, 1)
    stage_out(0, 0)
    stage_act(1, 1)
    stage_act(0, 2)
    stage_out(1, 0)
    store_tokens()
    stage_act(1, 3)
    stage_out(0, 1)
    stage_act(1, 2)
    stage_out(0, 3)
    stage_out(1, 1)
    stage_out(0, 2)
    store_acts(0)
    stage_z(0, 0)
    stage_out(1, 3)
    stage_z(1, 0)
    stage_z(0, 1)
    stage_out(1, 2)
    store_acts(1)
    stage_z(0, 3)
    stage_z(1, 1)
    stage_z(0, 2)
    stage_z(1, 3)
    stage_z(1, 2)
    last(0, out_ref)
    last(1, back_ref)
    left(tok.at[0, :, 0, pl.ds(0, 3 * ROWS)], Z)
    left(tok.at[0, :, pl.ds(0, 3)], X)
    left(tok.at[0], CORE)
    left(other, WEIGHT)
    left(in_a, SUM_A)
    left(in_b, SUM_B)
    left(in_b, ACT_A)
    left(in_a, ACT_B)
    left(act_a, PASS_A)
    left(act_b, PASS_B)
    left(xin, OUT)
    left(zin.at[0, :, pl.ds(1, 3)], NEAR)
    left(zin.at[pl.ds(1, 3)], FAR)
    pltpu.make_async_copy(tok, tok, store_sem.at[0]).wait()
    pltpu.make_async_copy(act_a, act_a, store_sem.at[1]).wait()
    pltpu.make_async_copy(act_b, act_b, store_sem.at[2]).wait()


def grads_kernel(
    out_ref, back_ref, tok_ref, hidden_ref, backs_ref, out_copy, back_copy, gate_grad, up_grad, down_grad
):
    @pl.when(pl.program_id(0) == 0)
    def _():
        out_copy[...] = out_ref[...]
        back_copy[...] = back_ref[...]

    f = hidden_ref.shape[-1]
    tokens, cot = [tok_ref[i].reshape(-1, tok_ref.shape[-1]) for i in range(2)]
    both = contract_first(backs_ref[...].reshape(-1, 2 * f), tokens).astype(BF16)
    gate_grad[...] = both[:f]
    up_grad[...] = both[f:]
    down_grad[...] = contract_first(hidden_ref[...].reshape(-1, f), cot).astype(BF16)


def weight_grads(out, back, tok, hidden, backs):
    d, f = tok.shape[-1], hidden.shape[-1]
    tile = 1024
    whole = pl.BlockSpec(out.shape, lambda i: (0, 0))
    grad = pl.BlockSpec((f, tile), lambda i: (0, i))
    small = jax.ShapeDtypeStruct(out.shape, BF16)
    large = jax.ShapeDtypeStruct((f, d), BF16)
    return pl.pallas_call(
        grads_kernel,
        grid=(d // tile,),
        out_shape=[small, small, large, large, large],
        in_specs=[
            whole, whole,
            pl.BlockSpec(tok.shape[:-1] + (tile,), lambda i: (0,) * (tok.ndim - 1) + (i,)),
            pl.BlockSpec(hidden.shape, lambda i: (0,) * hidden.ndim),
            pl.BlockSpec(backs.shape, lambda i: (0,) * backs.ndim),
        ],
        out_specs=[whole, whole, grad, grad, grad],
        compiler_params=pltpu.CompilerParams(vmem_limit_bytes=56 * 2**20),
        name="grads",
    )(out, back, tok, hidden, backs)


def on_device(tokens_in, cotangent, w_gate, w_up, w_down):
    d, f = w_gate.shape
    half = d // 2
    piece = half // 4
    group = NX * ROWS
    share = group // NY
    tokens = NQ * group
    dma = pltpu.SemaphoreType.DMA
    vmem = pl.BlockSpec(memory_space=pltpu.VMEM)
    hbm = pl.BlockSpec(memory_space=pltpu.HBM)
    out, back, tok, hidden, backs = pl.pallas_call(
        block_kernel,
        out_shape=[
            jax.ShapeDtypeStruct((4, d), BF16),
            jax.ShapeDtypeStruct((4, d), BF16),
            jax.ShapeDtypeStruct((2, NQ, group, d), BF16),
            jax.ShapeDtypeStruct((NQ, NY, share, f), BF16),
            jax.ShapeDtypeStruct((NQ, NY, share, 2 * f), BF16),
        ],
        in_specs=[hbm] * 5,
        out_specs=[vmem, vmem, hbm, hbm, hbm],
        scratch_shapes=[
            pltpu.VMEM((2, 2, NQ, group, half), BF16),
            pltpu.VMEM((2, 3, f, half), BF16),
            pltpu.VMEM((3, f, half), BF16),
            pltpu.VMEM((NQ, NY, share, 2 * f), F32),
            pltpu.VMEM((NQ, NY, share, f), F32),
            pltpu.VMEM((NQ, NY, share, 2 * f), BF16),
            pltpu.VMEM((NQ, NY, share, f), BF16),
            pltpu.VMEM((NQ, NY - 1, share, 2 * f), BF16),
            pltpu.VMEM((NQ, NY - 1, share, f), BF16),
            pltpu.VMEM((NQ, NY, share, f), BF16),
            pltpu.VMEM((NQ, NY, share, 2 * f), BF16),
            pltpu.VMEM((NQ, NY, share, f), BF16),
            pltpu.VMEM((NQ, NY, share, 2 * f), BF16),
            pltpu.VMEM((NQ, 2, ROWS, half), F32),
            pltpu.VMEM((NQ, 2, NX - 1, ROWS, half), BF16),
            pltpu.VMEM((NQ, 2, NX - 1, ROWS, half), BF16),
            pltpu.VMEM((NQ, 2, 4, ROWS, piece), F32),
            pltpu.VMEM((NQ, 2, 4, ROWS, piece), BF16),
            pltpu.VMEM((NQ, 2, 4, ROWS, piece), BF16),
            dma((3,)),
            dma((3,)),
            dma((13,)),
            dma((1,)),
            dma((2, NQ)),
            dma((2, NQ)),
            dma((2, NQ)),
            dma((2, NQ)),
            dma((2, NQ)),
            dma((2, NQ)),
            dma((2, NQ)),
            dma((2, NQ)),
        ],
        compiler_params=pltpu.CompilerParams(
            collective_id=0, has_side_effects=True, vmem_limit_bytes=56 * 2**20
        ),
        cost_estimate=pl.CostEstimate(flops=12 * tokens * d * f, bytes_accessed=6 * d * f, transcendentals=tokens * f),
        name="block",
    )(tokens_in, cotangent, w_gate.T, w_up.T, w_down)
    out, back, gate_grad, up_grad, down_grad = weight_grads(out, back, tok, hidden, backs)
    return (out, back, gate_grad.T, up_grad.T, down_grad)


def solution(mesh):
    return jax.shard_map(
        on_device,
        mesh=mesh,
        in_specs=(
            P("rows", "depth"),
            P("rows", "depth"),
            P("depth", ("rows", "cols")),
            P("depth", ("rows", "cols")),
            P(("rows", "cols"), "depth"),
        ),
        out_specs=(
            P(("rows", "cols"), "depth"),
            P(("rows", "cols"), "depth"),
            P("depth", ("rows", "cols")),
            P("depth", ("rows", "cols")),
            P(("rows", "cols"), "depth"),
        ),
        check_vma=False,
    )
```

time: 491 us -> 58.4 us (0.12)
  blocking collectives: 291 us -> 0 us
  waiting for transfers between devices: 159 us -> 0 us
  Pallas kernels: 0 us -> 57.6 us
  matrix products: 18.9 us -> 0 us
  between operations: 14.5 us -> 0.64 us
    unnamed x1 -> x0, blocking collectives: 291 us -> none
    all_gather x2 -> x0, waiting for transfers between devices: 107 us -> none  [the longest x1 57.8 us: on_device(): lax.all_gather(tokens_in, 'rows', axis=0, tiled=True)]
    pallas_call x0 -> x2, Pallas kernels: none -> 57.6 us  [the longest x1 53 us: on_device(): pl.pallas_call(block_kernel, out_shape=[jax.ShapeDtypeStruct((4, d), BF16...]
    psum x1 -> x0, waiting for transfers between devices: 50.4 us -> none  [on_device(): gate, up = lax.psum((gate_part, up_part), 'depth')]
    dot_general x9 -> x0, matrix products: 18.9 us -> none  [the longest x3 6.56 us: contract_first(): lax.dot_general(left, right, (((0,), (0,)), ((), ())), preferred_element_...]
  transfers between devices with their start and end apart: 3 -> 0, of which waited for: 3 -> 0; matrix products, arithmetic and copies ran while one was open for 1% -> 0% of each run, Pallas kernels for 0% -> 0%
where the time goes in v5:
time: 58.4 us; the launch traced here: 58.3 us
  Pallas kernels  57.6 us (99%)
  between operations  0.64 us (1%)
    pallas_call x1, Pallas kernels, on_device(): pl.pallas_call(block_kernel, out_shape=[jax.ShapeDtypeStruct((4, d), BF16...  53 us
    pallas_call x1, Pallas kernels, weight_grads(): pl.pallas_call(grads_kernel, grid=(d // tile,), out_shape=[small, small,...  4.62 us

profile of v5, /device:TPU:1, one launch (start us, length us, event | category | flops | bytes accessed | tf_op | source)
XLA Modules:
  0.0 58.3 jit_solution(4176115890160215742)
XLA Ops:
  0.6 53.0 %block.1 = (bf16[4,2048]{1,0:T(4,128)(2,1)}, bf16[4,2048]{1,0:T(4,128)(2,1)}, bf16[2,4,64,2048]{3,2,1,0:T(8,128)(2,1)}, bf16[4,4,16,448]{3,2,1,0:T(8,128)(2,1)}, bf16[4,4,16,896]{3,2,1,0:T(8,128)(2,1)}) custom-call(bf16[16,2048]{1,0:T(8,128)(2,1)} %tokens_ref.1, bf16[16,2048]{1,0:T(8,128)(2,1)} %cot_ref.1, bf16[448,2048]{1,0:T(8,128)(2,1)} %bitcast.4, ...), custom_call_target="tpu_custom_call" | custom-call | flops 2818572288 | bytes 5505024 | tf_op jit(solution)/shard_map/block/pallas_call | solution.py:353
  53.6 4.6 %grads.1 = (bf16[4,2048]{1,0:T(4,128)(2,1)}, bf16[4,2048]{1,0:T(4,128)(2,1)}, bf16[448,2048]{1,0:T(8,128)(2,1)}, bf16[448,2048]{1,0:T(8,128)(2,1)}, bf16[448,2048]{1,0:T(8,128)(2,1)}) custom-call(bf16[4,2048]{1,0:T(4,128)(2,1)} %get-tuple-element.15.out_ref, bf16[4,2048]{1,0:T(4,128)(2,1)} %get-tuple-element.16.back_ref, ...), custom_call_target="tpu_custom_call" | custom-call | tf_op jit(solution)/shard_map/grads/pallas_call | solution.py:327

commit v6 on v5

--- a/solution.py
+++ b/solution.py
@@ -124,8 +124,8 @@
     rows = NX * ROWS
     share = rows // NY
 
-    def stage_mm(a, n, h):
-        if n == 0 and a == 0:
+    def stage_mm(a, n, h, first):
+        if first:
             pltpu.make_async_copy(held.at[h], held.at[h], load_sem.at[h]).wait()
         if h:
             arrived(tok.at[1, a, n], cr.at[a, n])
@@ -155,23 +155,20 @@
             act_b[n, y] = jnp.concatenate([gate_back, total * gate * sigma], axis=1).astype(BF16)
         for d in (1, 3, 2):
             send(acts[a].at[n, y], acts[a].at[n, y], ACT_A + a, hr.at[a, n], at(dy=d))
-        send(acts[a].at[n, y], acts_other[a].at[n, y], PASS_A + a, kr.at[a, n], neighbour)
-
-    def stage_out(a, n):
+
+    def stage_pass(a, n):
         arrived(parts_in[1 - a].at[n], hr.at[a, n])
-        for p in (1, 3, 2):
-            place = lax.rem(y + p, NY)
-            send(acts[a].at[n, place], acts_other[a].at[n, place], PASS_A + a, kr.at[a, n], neighbour)
-
+        send(acts[a].at[n], acts_other[a].at[n], PASS_A + a, kr.at[a, n], neighbour)
+
+    def stage_out(a, n, first):
         def output(ref, w):
             left_side = ref[n].reshape(rows, -1)
             return matmul(left_side, w[0:2].reshape(2 * f, half) if a else w[2])
 
-        mine = output(acts[a], held.at[0])
-        if n == 0 and a == 0:
+        if first:
             arrived(other, wr.at[0])
         arrived(acts_other[a].at[n], kr.at[a, n])
-        value = (mine + output(acts_other[a], other)).reshape(NX, ROWS, half)
+        value = (output(acts[a], held.at[0]) + output(acts_other[a], other)).reshape(NX, ROWS, half)
         own[n, a] = value[0]
         xsend[n, a] = value[1:].astype(BF16)
         for d in (1, 3, 2):
@@ -221,66 +218,74 @@
 
     stage_z_in(0)
     stage_x(0, 0)
+    stage_weights()
+    stage_x(1, 0)
     stage_z_in(1)
-    stage_x(1, 0)
     stage_x(0, 1)
+    stage_x(0, 3)
     stage_core(0, 0)
-    stage_mm(0, 0, 0)
-    stage_x(0, 3)
-    stage_mm(0, 0, 1)
     stage_core(1, 0)
     stage_x(0, 2)
-    stage_x(1, 1)
-    stage_mm(1, 0, 0)
-    stage_mm(1, 0, 1)
+    stage_mm(0, 0, 0, True)
+    stage_mm(0, 0, 1, True)
     stage_x(1, 3)
     stage_core(0, 1)
-    stage_mm(0, 1, 0)
+    stage_mm(1, 0, 0, False)
+    stage_mm(0, 1, 0, False)
+    stage_mm(1, 0, 1, False)
     stage_x(1, 2)
     stage_core(0, 3)
-    stage_mm(0, 1, 1)
-    stage_mm(0, 3, 0)
+    stage_mm(0, 1, 1, False)
+    stage_x(1, 1)
+    stage_mm(0, 3, 0, False)
+    stage_core(0, 2)
+    stage_mm(0, 3, 1, False)
+    stage_mm(0, 2, 0, False)
+    stage_core(1, 3)
+    stage_mm(0, 2, 1, False)
+    stage_mm(1, 3, 0, False)
+    stage_core(1, 2)
     stage_act(0, 0)
-    stage_mm(0, 3, 1)
-    stage_core(0, 2)
+    stage_mm(1, 2, 0, False)
+    stage_act(0, 1)
+    stage_mm(1, 2, 1, False)
     stage_core(1, 1)
-    stage_weights()
+    stage_mm(1, 1, 0, False)
+    stage_mm(1, 3, 1, False)
+    stage_act(0, 3)
+    stage_act(0, 2)
+    stage_mm(1, 1, 1, False)
+    store_tokens()
+    stage_pass(0, 0)
+    stage_pass(0, 1)
+    stage_act(1, 2)
+    stage_out(0, 0, True)
+    stage_act(1, 3)
+    stage_out(0, 1, False)
+    stage_pass(0, 2)
+    stage_pass(0, 3)
+    stage_act(1, 1)
     stage_act(1, 0)
-    stage_mm(0, 2, 0)
-    stage_mm(0, 2, 1)
-    stage_mm(1, 1, 0)
-    stage_mm(1, 1, 1)
-    stage_core(1, 3)
-    stage_act(0, 1)
-    stage_mm(1, 3, 0)
-    stage_mm(1, 3, 1)
-    stage_core(1, 2)
-    stage_act(0, 3)
-    stage_mm(1, 2, 0)
-    stage_mm(1, 2, 1)
-    stage_out(0, 0)
-    stage_act(1, 1)
-    stage_act(0, 2)
-    stage_out(1, 0)
-    store_tokens()
-    stage_act(1, 3)
-    stage_out(0, 1)
-    stage_act(1, 2)
-    stage_out(0, 3)
-    stage_out(1, 1)
-    stage_out(0, 2)
+    stage_out(0, 2, False)
+    stage_pass(1, 2)
+    stage_out(0, 3, False)
+    stage_pass(1, 3)
+    stage_z(0, 0)
+    stage_out(1, 2, False)
+    stage_pass(1, 1)
+    stage_out(1, 3, False)
+    stage_pass(1, 0)
+    stage_out(1, 1, False)
+    stage_z(0, 2)
+    stage_out(1, 0, False)
     store_acts(0)
-    stage_z(0, 0)
-    stage_out(1, 3)
+    store_acts(1)
+    stage_z(0, 1)
+    stage_z(1, 2)
+    stage_z(0, 3)
+    stage_z(1, 3)
+    stage_z(1, 1)
     stage_z(1, 0)
-    stage_z(0, 1)
-    stage_out(1, 2)
-    store_acts(1)
-    stage_z(0, 3)
-    stage_z(1, 1)
-    stage_z(0, 2)
-    stage_z(1, 3)
-    stage_z(1, 2)
     last(0, out_ref)
     last(1, back_ref)
     left(tok.at[0, :, 0, pl.ds(0, 3 * ROWS)], Z)

time: 58.4 us -> 54.7 us (0.937)
  Pallas kernels: 57.6 us -> 53.9 us
    pallas_call x1, Pallas kernels: 53 us -> 49.3 us  [on_device(): pl.pallas_call(block_kernel, out_shape=[jax.ShapeDtypeStruct((4, d), BF16...]
where the time goes in v6:
time: 54.7 us; the launch traced here: 54.5 us
  Pallas kernels  53.9 us (99%)
  between operations  0.64 us (1%)
    pallas_call x1, Pallas kernels, on_device(): pl.pallas_call(block_kernel, out_shape=[jax.ShapeDtypeStruct((4, d), BF16...  49.3 us
    pallas_call x1, Pallas kernels, weight_grads(): pl.pallas_call(grads_kernel, grid=(d // tile,), out_shape=[small, small,...  4.62 us

profile of v6, /device:TPU:1, one launch (start us, length us, event | category | flops | bytes accessed | tf_op | source)
XLA Modules:
  0.0 54.5 jit_solution(18367903152299559141)
XLA Ops:
  0.6 49.3 %block.1 = (bf16[4,2048]{1,0:T(4,128)(2,1)}, bf16[4,2048]{1,0:T(4,128)(2,1)}, bf16[2,4,64,2048]{3,2,1,0:T(8,128)(2,1)}, bf16[4,4,16,448]{3,2,1,0:T(8,128)(2,1)}, bf16[4,4,16,896]{3,2,1,0:T(8,128)(2,1)}) custom-call(bf16[16,2048]{1,0:T(8,128)(2,1)} %tokens_ref.1, bf16[16,2048]{1,0:T(8,128)(2,1)} %cot_ref.1, bf16[448,2048]{1,0:T(8,128)(2,1)} %bitcast.4, ...), custom_call_target="tpu_custom_call" | custom-call | flops 2818572288 | bytes 5505024 | tf_op jit(solution)/shard_map/block/pallas_call | solution.py:358
  49.9 4.6 %grads.1 = (bf16[4,2048]{1,0:T(4,128)(2,1)}, bf16[4,2048]{1,0:T(4,128)(2,1)}, bf16[448,2048]{1,0:T(8,128)(2,1)}, bf16[448,2048]{1,0:T(8,128)(2,1)}, bf16[448,2048]{1,0:T(8,128)(2,1)}) custom-call(bf16[4,2048]{1,0:T(4,128)(2,1)} %get-tuple-element.15.out_ref, bf16[4,2048]{1,0:T(4,128)(2,1)} %get-tuple-element.16.back_ref, ...), custom_call_target="tpu_custom_call" | custom-call | tf_op jit(solution)/shard_map/grads/pallas_call | solution.py:332

commit v7 on v6

--- a/solution.py
+++ b/solution.py
@@ -35,10 +35,10 @@
 
 def block_kernel(
     tokens_ref, cot_ref, w_gate_ref, w_up_ref, w_down_ref,
-    out_ref, back_ref, tok_out, hidden_out, backs_out,
+    out_ref, back_ref, gate_grad, up_grad, down_grad,
     tok, held, other, sum_a, sum_b, part_a, part_b, in_a, in_b, act_a, act_b, other_a, other_b,
     own, xsend, xin, zf, zsend, zin,
-    load_sem, store_sem, sent, wr, zr, xr, cr, yr, hr, kr, ur, vr,
+    load_sem, sent, wr, zr, xr, cr, yr, hr, kr, ur, vr,
 ):
     r, c, y = lax.axis_index("rows"), lax.axis_index("cols"), lax.axis_index("depth")
     z_hi, x = r // NX, r % NX
@@ -48,7 +48,7 @@
     piece = half // 4
     weights = (w_gate_ref, w_up_ref, w_down_ref)
     sums, parts, parts_in = (sum_a, sum_b), (part_a, part_b), (in_a, in_b)
-    acts, acts_other, acts_out = (act_a, act_b), (other_a, other_b), (hidden_out, backs_out)
+    acts, acts_other = (act_a, act_b), (other_a, other_b)
 
     def at(dz=0, dx=0, lo=None, k=None, dy=0):
         lo = z_lo if lo is None else lo
@@ -208,13 +208,13 @@
                     totals[k][j * step:(j + 1) * step].astype(BF16)
                 )
 
-    def store_tokens():
-        for h in range(2):
-            for i in range(2):
-                pltpu.make_async_copy(tok.at[h, i], tok_out.at[i, :, :, features(h)], store_sem.at[0]).start()
-
-    def store_acts(a):
-        pltpu.make_async_copy(acts[a], acts_out[a], store_sem.at[1 + a]).start()
+    def stage_grad(i, h):
+        held_act = act_a[...] if i == 2 else act_b[:, :, :, i * f:(i + 1) * f]
+        left_side = held_act.reshape(NQ * rows, f)
+        for j in range(2):
+            right_side = tok[h, i // 2, :, :, j * half // 2:(j + 1) * half // 2].reshape(NQ * rows, half // 2)
+            place = pl.multiple_of((core + h) % 2 * half + j * half // 2, half // 2)
+            (gate_grad, up_grad, down_grad)[i][:, pl.ds(place, half // 2)] = contract_first(left_side, right_side).astype(BF16)
 
     stage_z_in(0)
     stage_x(0, 0)
@@ -224,69 +224,72 @@
     stage_x(0, 1)
     stage_x(0, 3)
     stage_core(0, 0)
+    stage_mm(0, 0, 0, True)
+    stage_x(1, 1)
+    stage_x(0, 2)
     stage_core(1, 0)
-    stage_x(0, 2)
-    stage_mm(0, 0, 0, True)
     stage_mm(0, 0, 1, True)
     stage_x(1, 3)
+    stage_mm(1, 0, 0, False)
     stage_core(0, 1)
-    stage_mm(1, 0, 0, False)
+    stage_mm(1, 0, 1, False)
+    stage_core(0, 3)
+    stage_mm(0, 3, 0, False)
     stage_mm(0, 1, 0, False)
-    stage_mm(1, 0, 1, False)
     stage_x(1, 2)
-    stage_core(0, 3)
     stage_mm(0, 1, 1, False)
-    stage_x(1, 1)
-    stage_mm(0, 3, 0, False)
+    stage_act(0, 0)
     stage_core(0, 2)
+    stage_act(1, 0)
+    stage_core(1, 1)
+    stage_mm(0, 2, 0, False)
+    stage_mm(1, 1, 0, False)
+    stage_mm(0, 2, 1, False)
+    stage_core(1, 3)
     stage_mm(0, 3, 1, False)
-    stage_mm(0, 2, 0, False)
-    stage_core(1, 3)
-    stage_mm(0, 2, 1, False)
+    stage_core(1, 2)
+    stage_mm(1, 2, 0, False)
     stage_mm(1, 3, 0, False)
-    stage_core(1, 2)
-    stage_act(0, 0)
-    stage_mm(1, 2, 0, False)
+    stage_pass(0, 0)
+    stage_mm(1, 2, 1, False)
     stage_act(0, 1)
-    stage_mm(1, 2, 1, False)
-    stage_core(1, 1)
-    stage_mm(1, 1, 0, False)
+    stage_mm(1, 1, 1, False)
+    stage_pass(1, 0)
+    stage_act(0, 2)
     stage_mm(1, 3, 1, False)
+    stage_out(0, 0, True)
     stage_act(0, 3)
-    stage_act(0, 2)
-    stage_mm(1, 1, 1, False)
-    store_tokens()
-    stage_pass(0, 0)
+    stage_act(1, 2)
     stage_pass(0, 1)
-    stage_act(1, 2)
-    stage_out(0, 0, True)
+    stage_out(1, 0, False)
+    stage_act(1, 1)
+    stage_pass(0, 2)
+    stage_out(0, 1, False)
     stage_act(1, 3)
-    stage_out(0, 1, False)
-    stage_pass(0, 2)
     stage_pass(0, 3)
-    stage_act(1, 1)
-    stage_act(1, 0)
     stage_out(0, 2, False)
+    stage_grad(2, 0)
     stage_pass(1, 2)
     stage_out(0, 3, False)
+    stage_z(0, 0)
+    stage_pass(1, 1)
+    stage_out(1, 2, False)
     stage_pass(1, 3)
-    stage_z(0, 0)
-    stage_out(1, 2, False)
-    stage_pass(1, 1)
+    stage_out(1, 1, False)
     stage_out(1, 3, False)
-    stage_pass(1, 0)
-    stage_out(1, 1, False)
+    stage_z(0, 1)
     stage_z(0, 2)
-    stage_out(1, 0, False)
-    store_acts(0)
-    store_acts(1)
-    stage_z(0, 1)
+    stage_grad(0, 1)
+    stage_z(0, 3)
     stage_z(1, 2)
-    stage_z(0, 3)
+    stage_z(1, 1)
+    stage_grad(2, 1)
     stage_z(1, 3)
-    stage_z(1, 1)
     stage_z(1, 0)
+    stage_grad(1, 1)
+    stage_grad(1, 0)
     last(0, out_ref)
+    stage_grad(0, 0)
     last(1, back_ref)
     left(tok.at[0, :, 0, pl.ds(0, 3 * ROWS)], Z)
     left(tok.at[0, :, pl.ds(0, 3)], X)
@@ -301,48 +304,28 @@
     left(xin, OUT)
     left(zin.at[0, :, pl.ds(1, 3)], NEAR)
     left(zin.at[pl.ds(1, 3)], FAR)
-    pltpu.make_async_copy(tok, tok, store_sem.at[0]).wait()
-    pltpu.make_async_copy(act_a, act_a, store_sem.at[1]).wait()
-    pltpu.make_async_copy(act_b, act_b, store_sem.at[2]).wait()
-
-
-def grads_kernel(
-    out_ref, back_ref, tok_ref, hidden_ref, backs_ref, out_copy, back_copy, gate_grad, up_grad, down_grad
-):
-    @pl.when(pl.program_id(0) == 0)
-    def _():
-        out_copy[...] = out_ref[...]
-        back_copy[...] = back_ref[...]
-
-    f = hidden_ref.shape[-1]
-    tokens, cot = [tok_ref[i].reshape(-1, tok_ref.shape[-1]) for i in range(2)]
-    both = contract_first(backs_ref[...].reshape(-1, 2 * f), tokens).astype(BF16)
-    gate_grad[...] = both[:f]
-    up_grad[...] = both[f:]
-    down_grad[...] = contract_first(hidden_ref[...].reshape(-1, f), cot).astype(BF16)
-
-
-def weight_grads(out, back, tok, hidden, backs):
-    d, f = tok.shape[-1], hidden.shape[-1]
-    tile = 1024
-    whole = pl.BlockSpec(out.shape, lambda i: (0, 0))
-    grad = pl.BlockSpec((f, tile), lambda i: (0, i))
-    small = jax.ShapeDtypeStruct(out.shape, BF16)
-    large = jax.ShapeDtypeStruct((f, d), BF16)
+
+
+def write_kernel(*refs):
+    n = len(refs) // 2
+    copies = [pltpu.make_async_copy(refs[i], refs[n + i], refs[-1].at[i]) for i in range(n)]
+    for copy in copies:
+        copy.start()
+    for copy in copies:
+        copy.wait()
+
+
+def write_out(arrays):
+    n = len(arrays)
     return pl.pallas_call(
-        grads_kernel,
-        grid=(d // tile,),
-        out_shape=[small, small, large, large, large],
-        in_specs=[
-            whole, whole,
-            pl.BlockSpec(tok.shape[:-1] + (tile,), lambda i: (0,) * (tok.ndim - 1) + (i,)),
-            pl.BlockSpec(hidden.shape, lambda i: (0,) * hidden.ndim),
-            pl.BlockSpec(backs.shape, lambda i: (0,) * backs.ndim),
-        ],
-        out_specs=[whole, whole, grad, grad, grad],
-        compiler_params=pltpu.CompilerParams(vmem_limit_bytes=56 * 2**20),
-        name="grads",
-    )(out, back, tok, hidden, backs)
+        write_kernel,
+        out_shape=[jax.ShapeDtypeStruct(v.shape, v.dtype) for v in arrays],
+        in_specs=[pl.BlockSpec(memory_space=pl.ANY)] * n,
+        out_specs=[pl.BlockSpec(memory_space=pl.ANY)] * n,
+        scratch_shapes=[pltpu.SemaphoreType.DMA((n,))],
+        compiler_params=pltpu.CompilerParams(vmem_limit_bytes=2**20),
+        name="write",
+    )(*arrays)
 
 
 def on_device(tokens_in, cotangent, w_gate, w_up, w_down):
@@ -355,17 +338,17 @@
     dma = pltpu.SemaphoreType.DMA
     vmem = pl.BlockSpec(memory_space=pltpu.VMEM)
     hbm = pl.BlockSpec(memory_space=pltpu.HBM)
-    out, back, tok, hidden, backs = pl.pallas_call(
+    results = pl.pallas_call(
         block_kernel,
         out_shape=[
             jax.ShapeDtypeStruct((4, d), BF16),
             jax.ShapeDtypeStruct((4, d), BF16),
-            jax.ShapeDtypeStruct((2, NQ, group, d), BF16),
-            jax.ShapeDtypeStruct((NQ, NY, share, f), BF16),
-            jax.ShapeDtypeStruct((NQ, NY, share, 2 * f), BF16),
+            jax.ShapeDtypeStruct((f, d), BF16),
+            jax.ShapeDtypeStruct((f, d), BF16),
+            jax.ShapeDtypeStruct((f, d), BF16),
         ],
         in_specs=[hbm] * 5,
-        out_specs=[vmem, vmem, hbm, hbm, hbm],
+        out_specs=[vmem] * 5,
         scratch_shapes=[
             pltpu.VMEM((2, 2, NQ, group, half), BF16),
             pltpu.VMEM((2, 3, f, half), BF16),
@@ -387,7 +370,6 @@
             pltpu.VMEM((NQ, 2, 4, ROWS, piece), BF16),
             pltpu.VMEM((NQ, 2, 4, ROWS, piece), BF16),
             dma((3,)),
-            dma((3,)),
             dma((13,)),
             dma((1,)),
             dma((2, NQ)),
@@ -400,12 +382,15 @@
             dma((2, NQ)),
         ],
         compiler_params=pltpu.CompilerParams(
-            collective_id=0, has_side_effects=True, vmem_limit_bytes=56 * 2**20
+            collective_id=0, has_side_effects=True, vmem_limit_bytes=40 * 2**20
         ),
         cost_estimate=pl.CostEstimate(flops=12 * tokens * d * f, bytes_accessed=6 * d * f, transcendentals=tokens * f),
         name="block",
-    )(tokens_in, cotangent, w_gate.T, w_up.T, w_down)
-    out, back, gate_grad, up_grad, down_grad = weight_grads(out, back, tok, hidden, backs)
+    )(*[
+        pltpu.with_memory_space_constraint(v, pltpu.HBM)
+        for v in (tokens_in, cotangent, w_gate.T, w_up.T, w_down)
+    ])
+    out, back, gate_grad, up_grad, down_grad = write_out(results)
     return (out, back, gate_grad.T, up_grad.T, down_grad)
 
 

time: 54.7 us -> 53.2 us (0.973)
  Pallas kernels: 53.9 us -> 52.4 us
    pallas_call x1, Pallas kernels: 4.62 us -> 2.49 us  [write_out(): pl.pallas_call(write_kernel, out_shape=[jax.ShapeDtypeStruct(v.shape, v.d...]
    pallas_call x1, Pallas kernels: 49.3 us -> 49.9 us  [on_device(): pl.pallas_call(block_kernel, out_shape=[jax.ShapeDtypeStruct((4, d), BF16...]
where the time goes in v7:
time: 53.2 us; the launch traced here: 53.1 us
  Pallas kernels  52.4 us (98%)
  between operations  0.64 us (1%)
    pallas_call x1, Pallas kernels, on_device(): pl.pallas_call(block_kernel, out_shape=[jax.ShapeDtypeStruct((4, d), BF16...  49.9 us
    pallas_call x1, Pallas kernels, write_out(): pl.pallas_call(write_kernel, out_shape=[jax.ShapeDtypeStruct(v.shape, v.d...  2.49 us

profile of v7, /device:TPU:1, one launch (start us, length us, event | category | flops | bytes accessed | tf_op | source)
XLA Modules:
  0.0 53.1 jit_solution(2313770293935688876)
XLA Ops:
  0.6 49.9 %block.1 = (bf16[4,2048]{1,0:T(4,128)(2,1)S(1)}, bf16[4,2048]{1,0:T(4,128)(2,1)S(1)}, bf16[448,2048]{1,0:T(8,128)(2,1)S(1)}, bf16[448,2048]{1,0:T(8,128)(2,1)S(1)}, bf16[448,2048]{1,0:T(8,128)(2,1)S(1)}) custom-call(bf16[16,2048]{1,0:T(8,128)(2,1)} %tokens_ref.1, bf16[16,2048]{1,0:T(8,128)(2,1)} %cot_ref.1, bf16[448,2048]{1,0:T(8,128)(2,1)} %bitcast.4, ...), custom_call_target="tpu_custom_call" | custom-call | flops 2818572288 | bytes 5505024 | tf_op jit(solution)/shard_map/block/pallas_call | solution.py:341
  50.6 2.5 %write.1 = (bf16[4,2048]{1,0:T(4,128)(2,1)}, bf16[4,2048]{1,0:T(4,128)(2,1)}, bf16[448,2048]{1,0:T(8,128)(2,1)}, bf16[448,2048]{1,0:T(8,128)(2,1)}, bf16[448,2048]{1,0:T(8,128)(2,1)}) custom-call(bf16[4,2048]{1,0:T(4,128)(2,1)S(1)} %get-tuple-element.15.refs_0_, bf16[4,2048]{1,0:T(4,128)(2,1)S(1)} %get-tuple-element.16.refs_1_, ...), custom_call_target="tpu_custom_call" | custom-call | tf_op jit(solution)/shard_map/write/pallas_call | solution.py:320

commit v8 on v7

--- a/solution.py
+++ b/solution.py
@@ -110,7 +110,7 @@
     def stage_x(a, q):
         if q:
             arrived(shard(a, q, 0), zr.at[a, q])
-        for d in (1, 3, 2):
+        for d in (2, 1, 3):
             send(shard(a, q, 0), shard(a, q, NX - d), X, xr.at[a, q], at(dx=d))
 
     def stage_core(a, q):
@@ -136,7 +136,7 @@
             parts[a][n] = term.astype(BF16)
         sums[a][n] = term
         if h:
-            for d in (1, 3, 2):
+            for d in (2, 1, 3):
                 to = lax.rem(y + d, NY)
                 send(parts[a].at[n, to], parts_in[a].at[n, NY - d - 1], SUM_A + a, yr.at[a, n], at(dy=d))
 
@@ -153,7 +153,7 @@
             sigma = jax.nn.sigmoid(gate)
             gate_back = total * up_sum * sigma * (1.0 + gate * (1.0 - sigma))
             act_b[n, y] = jnp.concatenate([gate_back, total * gate * sigma], axis=1).astype(BF16)
-        for d in (1, 3, 2):
+        for d in (2, 1, 3):
             send(acts[a].at[n, y], acts[a].at[n, y], ACT_A + a, hr.at[a, n], at(dy=d))
 
     def stage_pass(a, n):
@@ -171,7 +171,7 @@
         value = (output(acts[a], held.at[0]) + output(acts_other[a], other)).reshape(NX, ROWS, half)
         own[n, a] = value[0]
         xsend[n, a] = value[1:].astype(BF16)
-        for d in (1, 3, 2):
+        for d in (2, 1, 3):
             send(xsend.at[n, a, d - 1], xin.at[n, a, NX - d - 1], OUT, ur.at[a, n], at(dx=d))
 
     step = ROWS // 4
@@ -187,7 +187,7 @@
             for m, (lo, k) in enumerate(group):
                 send(zsend.at[0, a, lo * 2 + k], zin.at[0, a, m + 1], NEAR, vr.at[a, 0], at(lo=lo, k=k))
         else:
-            for differs in range(2):
+            for differs in (1, 0) if n == 3 else (0, 1):
                 lo = 1 - z_lo if differs else z_lo
                 back = 2 if n == 2 else 1 if differs == (n == 1) else 3
                 for k in range(2):
@@ -224,72 +224,72 @@
     stage_x(0, 1)
     stage_x(0, 3)
     stage_core(0, 0)
+    stage_core(1, 0)
+    stage_x(0, 2)
     stage_mm(0, 0, 0, True)
-    stage_x(1, 1)
-    stage_x(0, 2)
-    stage_core(1, 0)
     stage_mm(0, 0, 1, True)
     stage_x(1, 3)
+    stage_core(0, 1)
     stage_mm(1, 0, 0, False)
-    stage_core(0, 1)
+    stage_mm(0, 1, 0, False)
     stage_mm(1, 0, 1, False)
+    stage_x(1, 2)
     stage_core(0, 3)
+    stage_mm(0, 1, 1, False)
+    stage_x(1, 1)
     stage_mm(0, 3, 0, False)
-    stage_mm(0, 1, 0, False)
-    stage_x(1, 2)
-    stage_mm(0, 1, 1, False)
+    stage_core(0, 2)
+    stage_mm(0, 3, 1, False)
+    stage_mm(0, 2, 0, False)
+    stage_core(1, 3)
+    stage_mm(0, 2, 1, False)
+    stage_mm(1, 3, 0, False)
+    stage_core(1, 2)
     stage_act(0, 0)
-    stage_core(0, 2)
+    stage_mm(1, 2, 0, False)
+    stage_act(0, 1)
+    stage_mm(1, 2, 1, False)
+    stage_core(1, 1)
+    stage_mm(1, 1, 0, False)
+    stage_mm(1, 3, 1, False)
+    stage_act(0, 3)
+    stage_act(0, 2)
+    stage_mm(1, 1, 1, False)
+    stage_pass(0, 0)
+    stage_pass(0, 1)
+    stage_act(1, 2)
+    stage_out(0, 0, True)
+    stage_act(1, 3)
+    stage_out(0, 1, False)
+    stage_pass(0, 2)
+    stage_pass(0, 3)
+    stage_act(1, 1)
     stage_act(1, 0)
-    stage_core(1, 1)
-    stage_mm(0, 2, 0, False)
-    stage_mm(1, 1, 0, False)
-    stage_mm(0, 2, 1, False)
-    stage_core(1, 3)
-    stage_mm(0, 3, 1, False)
-    stage_core(1, 2)
-    stage_mm(1, 2, 0, False)
-    stage_mm(1, 3, 0, False)
-    stage_pass(0, 0)
-    stage_mm(1, 2, 1, False)
-    stage_act(0, 1)
-    stage_mm(1, 1, 1, False)
-    stage_pass(1, 0)
-    stage_act(0, 2)
-    stage_mm(1, 3, 1, False)
-    stage_out(0, 0, True)
-    stage_act(0, 3)
-    stage_act(1, 2)
-    stage_pass(0, 1)
-    stage_out(1, 0, False)
-    stage_act(1, 1)
-    stage_pass(0, 2)
-    stage_out(0, 1, False)
-    stage_act(1, 3)
-    stage_pass(0, 3)
     stage_out(0, 2, False)
-    stage_grad(2, 0)
     stage_pass(1, 2)
     stage_out(0, 3, False)
+    stage_pass(1, 3)
     stage_z(0, 0)
+    stage_out(1, 2, False)
     stage_pass(1, 1)
-    stage_out(1, 2, False)
-    stage_pass(1, 3)
+    stage_out(1, 3, False)
+    stage_pass(1, 0)
     stage_out(1, 1, False)
-    stage_out(1, 3, False)
+    stage_z(0, 2)
+    stage_out(1, 0, False)
     stage_z(0, 1)
-    stage_z(0, 2)
+    stage_z(0, 3)
+    stage_grad(2, 0)
+    stage_grad(2, 1)
+    stage_z(1, 2)
+    stage_grad(0, 0)
+    stage_z(1, 3)
+    stage_z(1, 1)
+    stage_z(1, 0)
     stage_grad(0, 1)
-    stage_z(0, 3)
-    stage_z(1, 2)
-    stage_z(1, 1)
-    stage_grad(2, 1)
-    stage_z(1, 3)
-    stage_z(1, 0)
+    stage_grad(1, 0)
     stage_grad(1, 1)
-    stage_grad(1, 0)
     last(0, out_ref)
-    stage_grad(0, 0)
     last(1, back_ref)
     left(tok.at[0, :, 0, pl.ds(0, 3 * ROWS)], Z)
     left(tok.at[0, :, pl.ds(0, 3)], X)

time: 53.2 us -> 51.4 us (0.966)
  Pallas kernels: 52.4 us -> 50.6 us
    pallas_call x1, Pallas kernels: 49.9 us -> 48.1 us  [on_device(): pl.pallas_call(block_kernel, out_shape=[jax.ShapeDtypeStruct((4, d), BF16...]
where the time goes in v8:
time: 51.4 us; the launch traced here: 51.3 us
  Pallas kernels  50.6 us (98%)
  between operations  0.64 us (1%)
    pallas_call x1, Pallas kernels, on_device(): pl.pallas_call(block_kernel, out_shape=[jax.ShapeDtypeStruct((4, d), BF16...  48.1 us
    pallas_call x1, Pallas kernels, write_out(): pl.pallas_call(write_kernel, out_shape=[jax.ShapeDtypeStruct(v.shape, v.d...  2.49 us

profile of v8, /device:TPU:1, one launch (start us, length us, event | category | flops | bytes accessed | tf_op | source)
XLA Modules:
  0.0 51.3 jit_solution(5241952387965223615)
XLA Ops:
  0.6 48.1 %block.1 = (bf16[4,2048]{1,0:T(4,128)(2,1)S(1)}, bf16[4,2048]{1,0:T(4,128)(2,1)S(1)}, bf16[448,2048]{1,0:T(8,128)(2,1)S(1)}, bf16[448,2048]{1,0:T(8,128)(2,1)S(1)}, bf16[448,2048]{1,0:T(8,128)(2,1)S(1)}) custom-call(bf16[16,2048]{1,0:T(8,128)(2,1)} %tokens_ref.1, bf16[16,2048]{1,0:T(8,128)(2,1)} %cot_ref.1, bf16[448,2048]{1,0:T(8,128)(2,1)} %bitcast.4, ...), custom_call_target="tpu_custom_call" | custom-call | flops 2818572288 | bytes 5505024 | tf_op jit(solution)/shard_map/block/pallas_call | solution.py:341
  48.8 2.5 %write.1 = (bf16[4,2048]{1,0:T(4,128)(2,1)}, bf16[4,2048]{1,0:T(4,128)(2,1)}, bf16[448,2048]{1,0:T(8,128)(2,1)}, bf16[448,2048]{1,0:T(8,128)(2,1)}, bf16[448,2048]{1,0:T(8,128)(2,1)}) custom-call(bf16[4,2048]{1,0:T(4,128)(2,1)S(1)} %get-tuple-element.15.refs_0_, bf16[4,2048]{1,0:T(4,128)(2,1)S(1)} %get-tuple-element.16.refs_1_, ...), custom_call_target="tpu_custom_call" | custom-call | tf_op jit(solution)/shard_map/write/pallas_call | solution.py:320

commit v9 on v8

--- a/solution.py
+++ b/solution.py
@@ -103,9 +103,9 @@
     steps = (0, up, 2, NQ - up)
 
     def stage_z_in(a):
-        send(shard(a, 0, 0), shard(a, 1, 0), Z, zr.at[a, 1], at(dz=up, lo=1 - z_lo))
-        send(shard(a, 0, 0), shard(a, 3, 0), Z, zr.at[a, 3], at(dz=up))
-        send(shard(a, 0, 0), shard(a, 2, 0), Z, zr.at[a, 2], at(dz=2, lo=1 - z_lo))
+        hops = [(1, at(dz=up, lo=1 - z_lo)), (3, at(dz=up)), (2, at(dz=2, lo=1 - z_lo))]
+        for q, to in hops[::-1] if a else hops:
+            send(shard(a, 0, 0), shard(a, q, 0), Z, zr.at[a, q], to)
 
     def stage_x(a, q):
         if q:

time: 51.4 us -> 51.6 us (level)
  no operation moved by 1% of the time
where the time goes in v9:
time: 51.6 us; the launch traced here: 51.5 us
  Pallas kernels  50.8 us (98%)
  between operations  0.64 us (1%)
    pallas_call x1, Pallas kernels, on_device(): pl.pallas_call(block_kernel, out_shape=[jax.ShapeDtypeStruct((4, d), BF16...  48.3 us
    pallas_call x1, Pallas kernels, write_out(): pl.pallas_call(write_kernel, out_shape=[jax.ShapeDtypeStruct(v.shape, v.d...  2.49 us

profile of v9, /device:TPU:1, one launch (start us, length us, event | category | flops | bytes accessed | tf_op | source)
XLA Modules:
  0.0 51.5 jit_solution(14713066201113776698)
XLA Ops:
  0.6 48.3 %block.1 = (bf16[4,2048]{1,0:T(4,128)(2,1)S(1)}, bf16[4,2048]{1,0:T(4,128)(2,1)S(1)}, bf16[448,2048]{1,0:T(8,128)(2,1)S(1)}, bf16[448,2048]{1,0:T(8,128)(2,1)S(1)}, bf16[448,2048]{1,0:T(8,128)(2,1)S(1)}) custom-call(bf16[16,2048]{1,0:T(8,128)(2,1)} %tokens_ref.1, bf16[16,2048]{1,0:T(8,128)(2,1)} %cot_ref.1, bf16[448,2048]{1,0:T(8,128)(2,1)} %bitcast.4, ...), custom_call_target="tpu_custom_call" | custom-call | flops 2818572288 | bytes 5505024 | tf_op jit(solution)/shard_map/block/pallas_call | solution.py:341
  49.0 2.5 %write.1 = (bf16[4,2048]{1,0:T(4,128)(2,1)}, bf16[4,2048]{1,0:T(4,128)(2,1)}, bf16[448,2048]{1,0:T(8,128)(2,1)}, bf16[448,2048]{1,0:T(8,128)(2,1)}, bf16[448,2048]{1,0:T(8,128)(2,1)}) custom-call(bf16[4,2048]{1,0:T(4,128)(2,1)S(1)} %get-tuple-element.15.refs_0_, bf16[4,2048]{1,0:T(4,128)(2,1)S(1)} %get-tuple-element.16.refs_1_, ...), custom_call_target="tpu_custom_call" | custom-call | tf_op jit(solution)/shard_map/write/pallas_call | solution.py:320
